TPU v7x, 32 devices: a whole 2x2x4 slice. The times are simulated.
32 devices in a mesh: dp: 2 (over x), seq: 16 (over z, y, core).
Axes of the slice: x: 2, y: 2, z: 4, core: 2. Of those that a mesh axis runs over, the one named last changes fastest.
Arguments:
- tokens: bfloat16 [8192, 512], P(('dp', 'seq')), parts along dimension 0, may hold values from -16 to 16
- globals_in: bfloat16 [256, 512], P('dp'), parts along dimension 0, may hold values from -16 to 16
- seg_ids: int32 [8192], P(('dp', 'seq')), parts along dimension 0, may hold values from 1 to 63, as said below
- global_table: int32 [256], P('dp'), parts along dimension 0, may hold values from 1 to 63
- w_qkv: bfloat16 [2, 512, 1536], replicated, may hold values from -1 to 1
- w_out: bfloat16 [2, 512, 512], replicated, may hold values from -0.25 to 0.25
- gain_local: float32 [2, 512], replicated, may hold values from 0.5 to 1.5
- gain_global: float32 [2, 512], replicated, may hold values from 0.5 to 1.5
- seg_bias: float32 [2, 8], replicated, may hold values from 2 to 5
Outputs:
- local_out: bfloat16 [8192, 512], P(('dp', 'seq')), parts along dimension 0
- global_out: bfloat16 [256, 512], P('dp'), parts along dimension 0
There are 2 independent parts, one for each index of `dp`. A program takes and returns all parts, laid end to end along the dimension named above; an argument that names none is the same for every part. Nothing has to cross between parts.
Inputs may be any that keep to these rules, and one draw needn't show every extreme that they name: `seg_ids`: the entity ids come in runs of 128 consecutive tokens (the first and last runs of a context are shorter).
All inputs are finite; a program needn't handle non-finite values.
Results may differ from a plain program's by a relative error of at most 0.006.
Values may be sent and summed in bfloat16 or wider, within the bound.
A program may use at most 192 MiB of HBM per device.

v0:
```python
import math

import jax
import jax.numpy as jnp
from jax import lax
from jax.sharding import PartitionSpec as P

RADIUS = 256
LAYERS = 2


masked_fill = -1e30


def with_halo(block, sides, width):
    for axis, dim in sides:
        count = lax.axis_size(axis)
        forward = [(i, i + 1) for i in range(count - 1)]
        backward = [(target, source) for source, target in forward]
        low = lax.ppermute(
            lax.slice_in_dim(block, block.shape[dim] - width, None, axis=dim), axis, forward
        )
        high = lax.ppermute(lax.slice_in_dim(block, 0, width, axis=dim), axis, backward)
        block = jnp.concatenate([low, block, high], axis=dim)
    return block


def layer_norm(values, gain):
    average = jnp.mean(values, axis=-1, keepdims=True)
    centered = values - average
    variance = jnp.mean(centered * centered, axis=-1, keepdims=True)
    return (centered * lax.rsqrt(variance + 1e-05) * gain).astype(jnp.bfloat16)


def window_attend(
    queries, keys_ext, values_ext, seg_rows, seg_ext, valid, gkeys, gvalues, bias, scaling
):
    rows = queries.shape[0]
    span = keys_ext.shape[0]
    radius = (span - rows) // 2
    scores = (
        jnp.einsum("thd,shd->hts", queries, keys_ext, preferred_element_type=jnp.float32) * scaling
    )
    offset = (
        jnp.arange(span, dtype=jnp.int32)[None, :]
        - radius
        - jnp.arange(rows, dtype=jnp.int32)[:, None]
    )
    allowed = (jnp.abs(offset) <= radius) & valid[None, :]
    same = (seg_rows[:, None] == seg_ext[None, :]).astype(jnp.float32)
    scores = scores + bias[:, None, None] * same[None]
    scores = jnp.where(allowed[None], scores, masked_fill)
    gscores = (
        jnp.einsum("thd,ghd->htg", queries, gkeys, preferred_element_type=jnp.float32) * scaling
    )
    top = jnp.maximum(jnp.max(scores, axis=-1), jnp.max(gscores, axis=-1))
    probs = jnp.exp(scores - top[..., None])
    gprobs = jnp.exp(gscores - top[..., None])
    total = jnp.sum(probs, axis=-1) + jnp.sum(gprobs, axis=-1)
    mixed = jnp.einsum(
        "hts,shd->thd", probs.astype(jnp.bfloat16), values_ext, preferred_element_type=jnp.float32
    )
    mixed = mixed + jnp.einsum(
        "htg,ghd->thd", gprobs.astype(jnp.bfloat16), gvalues, preferred_element_type=jnp.float32
    )
    return (mixed / jnp.transpose(total)[:, :, None]).reshape(rows, -1).astype(jnp.bfloat16)


def partial_global(gqueries, keys_loc, values_loc, seg_rows, table, scaling):
    scores = (
        jnp.einsum("ghd,thd->ght", gqueries, keys_loc, preferred_element_type=jnp.float32) * scaling
    )
    member = (table[:, None] == seg_rows[None, :])[:, None, :]
    scores = jnp.where(member, scores, masked_fill)
    top = jnp.max(scores, axis=-1)
    probs = jnp.where(member, jnp.exp(scores - top[..., None]), jnp.float32(0.0))
    total = jnp.sum(probs, axis=-1)
    weighted = jnp.einsum(
        "ght,thd->ghd", probs, values_loc.astype(jnp.float32), precision=lax.Precision.HIGHEST
    )
    return (top, total, weighted)


def self_global(gqueries, gkeys, gvalues, scaling):
    scores = (
        jnp.einsum("ghd,khd->ghk", gqueries, gkeys, preferred_element_type=jnp.float32) * scaling
    )
    top = jnp.max(scores, axis=-1)
    probs = jnp.exp(scores - top[..., None])
    total = jnp.sum(probs, axis=-1)
    weighted = jnp.einsum(
        "ghk,khd->ghd", probs, gvalues.astype(jnp.float32), precision=lax.Precision.HIGHEST
    )
    return (top, total, weighted)


def combine_parts(first, second):
    top = jnp.maximum(first[0], second[0])
    factor_a = jnp.exp(first[0] - top)
    factor_b = jnp.exp(second[0] - top)
    total = first[1] * factor_a + second[1] * factor_b
    weighted = first[2] * factor_a[..., None] + second[2] * factor_b[..., None]
    return (top, total, weighted)


def per_device(
    tokens, globals_in, seg_ids, global_table, w_qkv, w_out, gain_local, gain_global, seg_bias
):
    rows = tokens.shape[0]
    width = tokens.shape[1]
    heads = seg_bias.shape[1]
    head_dim = width // heads
    globals_count = globals_in.shape[0]
    scaling = 1.0 / math.sqrt(head_dim)
    shard = lax.axis_index("seq")
    shards = lax.axis_size("seq")
    seg_ext = with_halo(seg_ids, (("seq", 0),), RADIUS)
    position = shard * rows - RADIUS + jnp.arange(rows + 2 * RADIUS, dtype=jnp.int32)
    valid = (position >= 0) & (position < shards * rows)
    stream = tokens.astype(jnp.float32)
    gstate = globals_in.astype(jnp.float32)
    for layer_no in range(LAYERS):
        weight_in = w_qkv[layer_no]
        normed = layer_norm(stream, gain_local[layer_no])
        gnormed = layer_norm(gstate, gain_global[layer_no])
        proj = jnp.dot(normed, weight_in, preferred_element_type=jnp.float32).astype(jnp.bfloat16)
        gproj = jnp.dot(gnormed, weight_in, preferred_element_type=jnp.float32).astype(jnp.bfloat16)
        kv_ext = with_halo(proj[:, width:], (("seq", 0),), RADIUS)
        queries = proj[:, :width].reshape(rows, heads, head_dim)
        keys_ext = kv_ext[:, :width].reshape(-1, heads, head_dim)
        values_ext = kv_ext[:, width:].reshape(-1, heads, head_dim)
        gqueries = gproj[:, :width].reshape(globals_count, heads, head_dim)
        gkeys = gproj[:, width : 2 * width].reshape(globals_count, heads, head_dim)
        gvalues = gproj[:, 2 * width :].reshape(globals_count, heads, head_dim)
        local_mix = window_attend(
            queries,
            keys_ext,
            values_ext,
            seg_ids,
            seg_ext,
            valid,
            gkeys,
            gvalues,
            seg_bias[layer_no],
            scaling,
        )
        top, total, weighted = partial_global(
            gqueries,
            proj[:, width : 2 * width].reshape(rows, heads, head_dim),
            proj[:, 2 * width :].reshape(rows, heads, head_dim),
            seg_ids,
            global_table,
            scaling,
        )
        top_all = lax.pmax(top, "seq")
        factor = jnp.exp(top - top_all)
        total_all, weighted_all = lax.psum((total * factor, weighted * factor[..., None]), "seq")
        outer = (top_all, total_all, weighted_all)
        inner = self_global(gqueries, gkeys, gvalues, scaling)
        merged = combine_parts(outer, inner)
        global_mix = (
            (merged[2] / merged[1][..., None]).reshape(globals_count, width).astype(jnp.bfloat16)
        )
        stream = stream + jnp.dot(local_mix, w_out[layer_no], preferred_element_type=jnp.float32)
        gstate = gstate + jnp.dot(global_mix, w_out[layer_no], preferred_element_type=jnp.float32)
    return (stream.astype(jnp.bfloat16), gstate.astype(jnp.bfloat16))


def solution(mesh):
    return jax.shard_map(
        per_device,
        mesh=mesh,
        in_specs=(
            P(("dp", "seq"), None),
            P("dp", None),
            P(("dp", "seq")),
            P("dp"),
            P(),
            P(),
            P(),
            P(),
            P(),
        ),
        out_specs=(P(("dp", "seq"), None), P("dp", None)),
        check_vma=False,
    )
```

profile of v0, /device:TPU:0, one launch (start us, length us, event | category | flops | bytes accessed | tf_op | source)
XLA Modules:
  0.0 376.3 jit_solution(2762046521243310557)
XLA Ops:
  7.3 0.8 fusion.140
  8.0 1.1 convert_reduce_fusion
  9.1 1.2 fusion.69
  10.3 2.1 convolution_convert_fusion.1
  12.4 0.9 slice.114
  13.3 3.2 collective-permute-start
  16.4 1.3 collective-permute-start.1
  17.7 4.4 %collective-permute-start.2 = (s32[256]{0:T(256)}, s32[256]{0:T(256)S(1)}, u32[]{:S(2)}, u32[]{:S(2)}) collective-permute-start(s32[256]{0:T(256)} %param.11), channel_id=1, source_target_pairs={{0,1},{1,2},{2,3},{3,4},{4,5},{5,6},{6,7},{7,8},{8,9},{9,10},{10,1... | collective-permute-start | bytes 3080 | tf_op jit(solution)/shard_map/ppermute | solution.py:20
  22.1 1.3 collective-permute-start.3
  24.0 1.8 convolution_convert_fusion.3
  25.8 0.7 fusion.139
  26.8 0.4 fusion.144
  27.2 34.9 %pmax.14 = f32[128,8]{0,1:T(8,128)S(1)} all-reduce(f32[128,8]{0,1:T(8,128)S(1)} %get-tuple-element.40), channel_id=1, replica_groups=mesh['dp'=2,'seq'=16] {'seq'}, use_global_device_ids=true, to_apply=%region_12.13 | all-reduce | flops 1024 | bytes 8192 | tf_op jit(solution)/shard_map/pmax | solution.py:155
  62.1 0.4 fusion.64
  62.6 1.6 fusion.41
  64.4 29.7 %psum.29 = f32[128,8]{0,1:T(8,128)S(1)} all-reduce(f32[128,8]{0,1:T(8,128)S(1)} %get-tuple-element.10), channel_id=1, replica_groups=mesh['dp'=2,'seq'=16] {'seq'}, use_global_device_ids=true, to_apply=%region_16.17 | all-reduce | flops 1024 | bytes 8192 | tf_op jit(solution)/shard_map/psum | solution.py:157
  95.1 0.9 fusion.66
  96.1 1.7 copy.45
  97.9 52.6 %all-reduce.3.cloned.1.call-done = f32[128,8,64]{0,2,1:T(8,128)} async-done(((f32[128,8,64]{0,2,1:T(8,128)}), f32[128,8,64]{0,2,1:T(8,128)}) %all-reduce.3.cloned.1.call-update) | async-done | bytes 262160 | tf_op jit(solution)/shard_map/psum | solution.py:157
  150.5 1.4 fusion.46
  152.0 1.2 fusion.145
  153.4 0.5 copy-done.4
  154.0 1.9 convolution_convert_fusion.2
  155.8 0.7 fusion.138
  156.7 1.1 copy.60
  157.8 1.7 copy.56
  159.9 0.7 copy-done.5
  160.6 1.5 pad_maximum_fusion
  162.0 1.3 fusion.135
  163.3 2.3 copy.43
  165.6 3.3 fusion.4
  169.2 1.5 fusion.74
  170.7 1.1 copy-done.1
  171.8 2.1 fusion
  173.9 1.4 copy.41
  175.3 5.1 %fusion.57 = bf16[256,8,64]{0,2,1:T(8,128)(2,1)S(1)} fusion(f32[8,64,256]{2,1,0:T(8,128)} %fusion.74, bf16[768,8,64]{0,2,1:T(8,128)(2,1)S(1)} %bitcast.153, f32[8,256,768]{2,1,0:T(8,128)} %copy-done.1, f32[8,256]{1,0:T(8,128)S(1)} %max.24, f32[256,768]{1,0:T(8,128)S(1)} %compare_convert_fusion, f32[8]{0:T(128)S(1)} %get-tuple-element.33, ...), kind=kOutput, calls=%fused_computation.69 | convolution fusion | flops 211156992 | bytes 8863776 | tf_op jit(solution)/shard_map/hts,shd->thd/dot_general | solution.py:60
  180.4 0.4 fusion.146
  181.1 0.6 convolution_convert_fusion
  181.7 0.8 fusion.136
  182.5 0.8 slice.120
  183.4 3.3 collective-permute-start.4
  186.6 1.3 collective-permute-start.5
  187.9 0.8 copy.59
  188.8 1.4 fusion.149
  190.2 33.5 %pmax.15 = f32[128,8]{0,1:T(8,128)S(1)} all-reduce(f32[128,8]{0,1:T(8,128)S(1)} %get-tuple-element.52), channel_id=1, replica_groups=mesh['dp'=2,'seq'=16] {'seq'}, use_global_device_ids=true, to_apply=%region_24.25 | all-reduce | flops 1024 | bytes 8192 | tf_op jit(solution)/shard_map/pmax | solution.py:155
  223.7 0.4 fusion.65
  224.1 29.7 %psum.31 = f32[128,8]{0,1:T(8,128)S(1)} all-reduce(f32[128,8]{0,1:T(8,128)S(1)} %get-tuple-element.5), channel_id=1, replica_groups=mesh['dp'=2,'seq'=16] {'seq'}, use_global_device_ids=true, to_apply=%region_28.29 | all-reduce | flops 1024 | bytes 8192 | tf_op jit(solution)/shard_map/psum | solution.py:157
  253.8 1.8 copy.58
  255.6 2.6 fusion.42
  258.2 1.8 copy.48
  260.0 1.3 fusion.147
  261.4 83.0 %all-reduce.5.cloned.1.call-done = f32[128,8,64]{0,2,1:T(8,128)} async-done(((f32[128,8,64]{0,2,1:T(8,128)}), f32[128,8,64]{0,2,1:T(8,128)}) %all-reduce.5.cloned.1.call-update) | async-done | bytes 262160 | tf_op jit(solution)/shard_map/psum | solution.py:157
  344.4 1.6 fusion.47
  345.9 1.9 fusion.45
  347.8 1.5 pad_maximum_fusion.1
  349.3 1.3 fusion.134
  350.6 2.3 copy.49
  352.9 3.4 fusion.5
  356.5 1.5 fusion.72
  358.0 1.1 copy-done
  359.1 2.8 fusion.2
  361.9 1.4 copy.47
  363.4 5.0 %fusion.51 = bf16[256,8,64]{0,2,1:T(8,128)(2,1)S(1)} fusion(f32[8,64,256]{2,1,0:T(8,128)} %fusion.72, bf16[768,8,64]{0,2,1:T(8,128)(2,1)S(1)} %bitcast.152, f32[8,256,768]{2,1,0:T(8,128)} %copy-done, f32[8,256]{1,0:T(8,128)S(1)} %max.26, f32[8]{0:T(128)S(1)} %copy-done.17, f32[256,768]{1,0:T(8,128)S(1)} %compare_convert_fusion, ...), kind=kOutput, calls=%fused_computation.67 | convolution fusion | flops 211156992 | bytes 8863776 | tf_op jit(solution)/shard_map/hts,shd->thd/dot_general | solution.py:60
  368.4 1.0 fusion.36
  (89 shorter events, 3.5 us)
Async XLA Ops:
  7.2 19.5 %copy-start.14 = (s32[256]{0:T(256)S(1)}, s32[256]{0:T(256)}, u32[]{:S(2)}) copy-start(s32[256]{0:T(256)} %param.11) | copy-start | bytes 3076
  7.2 16.4 %copy-start.15 = (f32[2,512]{1,0:T(2,128)S(1)}, f32[2,512]{1,0:T(2,128)}, u32[]{:S(2)}) copy-start(f32[2,512]{1,0:T(2,128)} %param.16) | copy-start | bytes 12292
  7.2 16.5 %copy-start.9 = (bf16[128,512]{1,0:T(8,128)(2,1)S(1)}, bf16[128,512]{1,0:T(8,128)(2,1)}, u32[]{:S(2)}) copy-start(bf16[128,512]{1,0:T(8,128)(2,1)} %param.10) | copy-start | bytes 393220
  7.2 19.5 %copy-start.19 = (s32[128]{0:T(128)S(1)}, s32[128]{0:T(128)}, u32[]{:S(2)}) copy-start(s32[128]{0:T(128)} %param.12) | copy-start | bytes 1540
  7.2 143.3 %all-reduce.3.cloned.1.call-start = ((), (), s32[]{:S(2)}) async-start(), calls=%async_computation | async-start | bytes 524288 | tf_op jit(solution)/shard_map/psum | solution.py:157
  13.3 146.6 %collective-permute-start = (bf16[256,1024]{1,0:T(8,128)(2,1)}, bf16[256,1024]{1,0:T(8,128)(2,1)}, u32[]{:S(2)}, u32[]{:S(2)}) collective-permute-start(bf16[256,1024]{1,0:T(8,128)(2,1)} %slice.114), channel_id=1, source_target_pairs={{0,1},{1,2},{2,3},{3,4},{4,5},{5,6},{6,7},{7,8},{8,9},{9,10},{10,1... | collective-permute-start | bytes 1572872 | tf_op jit(solution)/shard_map/ppermute | solution.py:20
  16.4 144.1 %collective-permute-start.1 = (bf16[256,1024]{1,0:T(8,128)(2,1)}, bf16[256,1024]{1,0:T(8,128)(2,1)}, u32[]{:S(2)}, u32[]{:S(2)}) collective-permute-start(bf16[256,1024]{1,0:T(8,128)(2,1)} %slice.114), channel_id=1, source_target_pairs={{1,0},{2,1},{3,2},{4,3},{5,4},{6,5},{7,6},{8,7},{9,8},{10,9},{11,1... | collective-permute-start | bytes 1572872 | tf_op jit(solution)/shard_map/ppermute | solution.py:23
  17.7 80.0 %collective-permute-start.2 = (s32[256]{0:T(256)}, s32[256]{0:T(256)S(1)}, u32[]{:S(2)}, u32[]{:S(2)}) collective-permute-start(s32[256]{0:T(256)} %param.11), channel_id=1, source_target_pairs={{0,1},{1,2},{2,3},{3,4},{4,5},{5,6},{6,7},{7,8},{8,9},{9,10},{10,1... | collective-permute-start | bytes 3080 | tf_op jit(solution)/shard_map/ppermute | solution.py:20
  22.1 75.6 %collective-permute-start.3 = (s32[256]{0:T(256)}, s32[256]{0:T(256)S(1)}, u32[]{:S(2)}, u32[]{:S(2)}) collective-permute-start(s32[256]{0:T(256)} %param.11), channel_id=1, source_target_pairs={{1,0},{2,1},{3,2},{4,3},{5,4},{6,5},{7,6},{8,7},{9,8},{10,9},{11,1... | collective-permute-start | bytes 3080 | tf_op jit(solution)/shard_map/ppermute | solution.py:23
  23.8 72.3 %copy-start.18 = (f32[2,8]{1,0:T(2,128)S(1)}, f32[2,8]{1,0:T(2,128)}, u32[]{:S(2)}) copy-start(f32[2,8]{1,0:T(2,128)} %param.17) | copy-start | bytes 196
  25.8 126.1 %copy-start.2 = (bf16[2,512,512]{2,1,0:T(8,128)(2,1)S(1)}, bf16[2,512,512]{2,1,0:T(8,128)(2,1)}, u32[]{:S(2)}) copy-start(bf16[2,512,512]{2,1,0:T(8,128)(2,1)} %param.14) | copy-start | bytes 3145732
  64.3 280.1 %all-reduce.5.cloned.1.call-start = ((), (), s32[]{:S(2)}) async-start(), calls=%async_computation.1 | async-start | bytes 524288 | tf_op jit(solution)/shard_map/psum | solution.py:157
  94.6 3.1 copy-start.11
  96.1 256.8 %copy-start.16 = (f32[8]{0:T(128)}, f32[8]{0:T(128)S(1)}, u32[]{:S(2)}) copy-start(f32[8]{0:T(128)S(1)} %get-tuple-element.32) | copy-start | bytes 100
  153.2 0.7 copy-start.4
  153.9 11.7 %copy-start.6 = (pred[256,768]{1,0:T(8,128)(4,1)S(1)}, pred[256,768]{1,0:T(8,128)(4,1)}, u32[]{:S(2)}) copy-start(pred[256,768]{1,0:T(8,128)(4,1)} %fusion.66) | copy-start | bytes 589828
  156.7 12.3 %copy-start.10 = (bf16[128,512]{0,1:T(8,128)(2,1)}, bf16[128,512]{0,1:T(8,128)(2,1)S(1)}, u32[]{:S(2)}) copy-start(bf16[128,512]{0,1:T(8,128)(2,1)S(1)} %copy.55) | copy-start | bytes 393220
  157.7 11.2 %copy-start.8 = (bf16[128,512]{0,1:T(8,128)(2,1)}, bf16[128,512]{0,1:T(8,128)(2,1)S(1)}, u32[]{:S(2)}) copy-start(bf16[128,512]{0,1:T(8,128)(2,1)S(1)} %copy.60) | copy-start | bytes 393220
  159.8 0.8 copy-start.5
  165.6 3.5 copy-start.13
  169.0 2.8 copy-start.1
  175.3 5.1 %copy-start.3 = (bf16[256,512]{1,0:T(8,128)(2,1)S(1)}, bf16[256,512]{1,0:T(8,128)(2,1)}, u32[]{:S(2)}) copy-start(bf16[256,512]{1,0:T(8,128)(2,1)} %param.9) | copy-start | bytes 786436
  175.3 5.7 %copy-start.20 = (bf16[2,512,1536]{2,1,0:T(8,128)(2,1)S(1)}, bf16[2,512,1536]{2,1,0:T(8,128)(2,1)}, u32[]{:S(2)}) copy-start(bf16[2,512,1536]{2,1,0:T(8,128)(2,1)} %param.13) | copy-start | bytes 9437188
  183.4 164.4 %collective-permute-start.4 = (bf16[256,1024]{1,0:T(8,128)(2,1)}, bf16[256,1024]{1,0:T(8,128)(2,1)}, u32[]{:S(2)}, u32[]{:S(2)}) collective-permute-start(bf16[256,1024]{1,0:T(8,128)(2,1)} %slice.120), channel_id=1, source_target_pairs={{0,1},{1,2},{2,3},{3,4},{4,5},{5,6},{6,7},{7,8},{8,9},{9,10},{10,1... | collective-permute-start | bytes 1572872 | tf_op jit(solution)/shard_map/ppermute | solution.py:20
  186.6 161.2 %collective-permute-start.5 = (bf16[256,1024]{1,0:T(8,128)(2,1)}, bf16[256,1024]{1,0:T(8,128)(2,1)}, u32[]{:S(2)}, u32[]{:S(2)}) collective-permute-start(bf16[256,1024]{1,0:T(8,128)(2,1)} %slice.120), channel_id=1, source_target_pairs={{1,0},{2,1},{3,2},{4,3},{5,4},{6,5},{7,6},{8,7},{9,8},{10,9},{11,1... | collective-permute-start | bytes 1572872 | tf_op jit(solution)/shard_map/ppermute | solution.py:23
  350.6 5.9 %copy-start.12 = (bf16[128,512]{0,1:T(8,128)(2,1)S(1)}, bf16[128,512]{0,1:T(8,128)(2,1)}, u32[]{:S(2)}) copy-start(bf16[128,512]{0,1:T(8,128)(2,1)} %copy.56) | copy-start | bytes 393220
  352.9 6.2 %copy-start.7 = (pred[256,768]{1,0:T(8,128)(4,1)S(1)}, pred[256,768]{1,0:T(8,128)(4,1)}, u32[]{:S(2)}) copy-start(pred[256,768]{1,0:T(8,128)(4,1)} %fusion.66) | copy-start | bytes 589828
  356.3 2.8 copy-start
  358.0 5.3 %copy-start.17 = (f32[8]{0:T(128)S(1)}, f32[8]{0:T(128)}, u32[]{:S(2)}) copy-start(f32[8]{0:T(128)} %copy-done.16) | copy-start | bytes 100
Sparse Core Ops, SparseCore 0:
  64.4 86.0 all-reduce.2
  258.3 86.0 all-reduce.4
where the time goes:
time: 377 us; the launch traced here: 376 us
  waiting for transfers between devices  136 us (36%)
  blocking collectives  128 us (34%)
  matrix products  42.2 us (11%)
  local copies, waits for them, and re-layouts  27.9 us (7%)
  starting transfers between devices  14.7 us (4%)
  between operations  14.7 us (4%)
  other arithmetic  13.3 us (4%)
    psum x2, waiting for transfers between devices, per_device(): lax.psum((total * factor, weighted * factor[..., None]), 'seq')  136 us
    pmax x2, blocking collectives, per_device(): top_all = lax.pmax(top, 'seq')  68.4 us
    psum x2, blocking collectives, per_device(): lax.psum((total * factor, weighted * factor[..., None]), 'seq')  59.4 us
    ppermute x3, starting transfers between devices, with_halo(): lax.ppermute(lax.slice_in_dim(block, block.shape[dim] - width, None, axis...  10.8 us
    dot_general x2, matrix products, window_attend(): jnp.einsum('hts,shd->thd', probs.astype(jnp.bfloat16), values_ext, prefer...  10.1 us
  transfers between devices with their start and end apart: 8, of which 2 were waited for; matrix products, arithmetic and copies ran while one was open for 8% of the time, Pallas kernels for 0%

commit v1 on v0

v1 whole, which is shorter than its diff:
```python
import functools

import jax
import jax.numpy as jnp
from jax import lax
from jax.experimental import pallas as pl
from jax.experimental.pallas import tpu as pltpu
from jax.sharding import PartitionSpec as P

LAYERS = 2
BLK = 128
GROWS = 8
NEG = -1e30
F32 = jnp.float32
BF16 = jnp.bfloat16
NT = (((1,), (1,)), ((), ()))


def norm_rows(values, gain):
    average = jnp.mean(values, axis=-1, keepdims=True)
    centered = values - average
    variance = jnp.mean(centered * centered, axis=-1, keepdims=True)
    return centered * lax.rsqrt(variance + 1e-05) * gain


def three_parts(x):
    hi = x.astype(BF16).astype(F32)
    rest = x - hi
    mid = rest.astype(BF16).astype(F32)
    return hi, mid, (rest - mid).astype(BF16).astype(F32)


def fold(rows):
    half = rows.shape[1] // 2
    return jnp.concatenate([rows[:, :half], rows[:, half:]], axis=0)


def kernel(
    n, owners, heads,
    tok_ref, glob_ref, seg_ref, table_ref, wqkv_hbm, wout_hbm, gl_ref, gg_ref, bias_ref,
    out_ref, gout_ref,
    wqkv, wout, wvt, xa, xh, seg_own, seg_halo,
    qe, qo, ks, vt, kh, vht, e_own, e_halo, e_glob,
    o_a, m_a, l_a, mixt, stream, gstate, gown, rs_src, rs_buf, ag_buf,
    w_sem, seg_send, seg_recv, h_send, h_recv, rs_send, rs_recv, ag_send, ag_recv,
):
    rows, width = tok_ref.shape
    gcount = glob_ref.shape[0]
    head_dim = width // heads
    me = lax.axis_index("seq")
    has_left = me > 0
    has_right = me < n - 1
    left = jnp.maximum(me - 1, 0)
    right = jnp.minimum(me + 1, n - 1)

    barrier = pltpu.get_barrier_semaphore()

    @pl.loop(1, n)
    def _(r):
        pl.semaphore_signal(
            barrier, inc=1, device_id={"seq": lax.rem(me + r, n)},
            device_id_type=pl.DeviceIdType.MESH,
        )

    wcopies = []
    for l in range(LAYERS):
        wcopies.append(pltpu.make_async_copy(wqkv_hbm.at[l], wqkv.at[l], w_sem.at[l]))
    wcopies.append(pltpu.make_async_copy(wout_hbm, wout, w_sem.at[LAYERS]))
    for c in wcopies:
        c.start()

    seg_own[...] = jnp.zeros(seg_own.shape, F32)
    seg_own[0:2, :] = seg_ref[...].astype(F32)

    @pl.when(jnp.logical_not(has_left))
    def _():
        seg_halo[0] = jnp.zeros(seg_halo.shape[1:], F32)
        for l in range(LAYERS):
            xh[l, 0:rows, :] = jnp.zeros((rows, width), BF16)

    @pl.when(jnp.logical_not(has_right))
    def _():
        seg_halo[1] = jnp.zeros(seg_halo.shape[1:], F32)
        for l in range(LAYERS):
            xh[l, rows : 2 * rows, :] = jnp.zeros((rows, width), BF16)

    stream[...] = tok_ref[...].astype(F32)
    xa[0, 0:rows, :] = norm_rows(stream[...], gl_ref[0:1, :]).astype(BF16)
    pl.semaphore_wait(barrier, n - 1)

    def remote(src, dst, ssem, rsem, target):
        return pltpu.make_async_remote_copy(
            src_ref=src, dst_ref=dst, send_sem=ssem, recv_sem=rsem,
            device_id={"seq": target}, device_id_type=pl.DeviceIdType.MESH,
        )

    def halo_to_right(l):
        return remote(
            xa.at[l, pl.ds(0, rows)], xh.at[l, pl.ds(0, rows)], h_send.at[l, 0], h_recv.at[l, 0], right
        )

    def halo_to_left(l):
        return remote(
            xa.at[l, pl.ds(0, rows)], xh.at[l, pl.ds(rows, rows)], h_send.at[l, 1], h_recv.at[l, 1], left
        )

    def seg_to_right():
        return remote(seg_own, seg_halo.at[0], seg_send.at[0], seg_recv.at[0], right)

    def seg_to_left():
        return remote(seg_own, seg_halo.at[1], seg_send.at[1], seg_recv.at[1], left)

    def send_halo(l):
        @pl.when(has_right)
        def _():
            halo_to_right(l).start()

        @pl.when(has_left)
        def _():
            halo_to_left(l).start()

    def wait_halo(l):
        @pl.when(has_left)
        def _():
            halo_to_right(l).wait_recv()

        @pl.when(has_right)
        def _():
            halo_to_left(l).wait_recv()

    send_halo(0)

    @pl.when(has_right)
    def _():
        seg_to_right().start()

    @pl.when(has_left)
    def _():
        seg_to_left().start()

    all_own = n == owners

    def only_owner(body):
        if all_own:
            body()
        else:
            pl.when(me < owners)(body)

    def others(count, body):
        if count == n:
            @pl.loop(1, n)
            def _(r):
                body(lax.rem(me + r, n))
        else:
            @pl.loop(0, count)
            def _(r):
                @pl.when(r != me)
                def _():
                    body(r)

    def rs_copy(l, target, source):
        return remote(
            rs_src.at[l, target], rs_buf.at[l, source], rs_send.at[l, target], rs_recv.at[l, source], target
        )

    def ag_copy(l, target, source):
        return remote(
            ag_buf.at[l, source], ag_buf.at[l, source], ag_send.at[l, target], ag_recv.at[l, source], target
        )

    gstate[...] = glob_ref[...].astype(F32)

    def take_own():
        gown[...] = gstate[pl.ds(me * GROWS, GROWS), :]

    only_owner(take_own)
    xa[0, rows : rows + gcount, :] = norm_rows(gstate[...], gg_ref[0:1, :]).astype(BF16)

    def down(row):
        return jnp.transpose(jnp.broadcast_to(row, (BLK, BLK)))

    for kb in range(2):
        column = down(seg_own[kb : kb + 1, :])
        for rb in range(2):
            row = jnp.broadcast_to(seg_own[rb : rb + 1, :], (BLK, BLK))
            e_own[rb, kb * BLK : (kb + 1) * BLK, :] = jnp.where(column == row, 1.0, 0.0).astype(F32)
        trow = jnp.broadcast_to(table_ref[...].astype(F32), (BLK, BLK))
        e_glob[kb * BLK : (kb + 1) * BLK, :] = jnp.where(column == trow, 0.0, NEG).astype(F32)
    first = jnp.where(me == 0, 0.0, NEG).astype(F32)
    e_glob[2 * BLK : 2 * BLK + gcount, :] = jnp.full((gcount, BLK), 0.0, F32) + first

    lane = lax.broadcasted_iota(jnp.int32, (1, width), 1)
    even = jnp.where(lax.rem(lane // head_dim, 2) == 0, 0.125, 0.0).astype(F32)
    odd = 0.125 - even

    pick = lax.broadcasted_iota(jnp.int32, (BLK, width), 0)
    head_of = lax.broadcasted_iota(jnp.int32, (BLK, width), 1) // head_dim

    def expander(base):
        hit = (pick == base + head_of) | (pick == base + 8 + head_of) | (pick == base + 16 + head_of)
        return jnp.where(hit, 1.0, 0.0).astype(F32).astype(BF16)

    def project(l, lo, count):
        x = xa[l, lo : lo + count, :]
        q = jnp.dot(x, wqkv[l, :, 0:width], preferred_element_type=F32)
        qe[lo : lo + count, :] = (q * even).astype(BF16)
        qo[lo : lo + count, :] = (q * odd).astype(BF16)
        ks[lo : lo + count, :] = jnp.dot(
            x, wqkv[l, :, width : 2 * width], preferred_element_type=F32
        ).astype(BF16)
        vt[:, lo : lo + count] = lax.dot_general(
            wvt[l], x, NT, preferred_element_type=F32
        ).astype(BF16)

    def attend(h, k_ref, v_ref, k0, count, q0, table):
        pair = pl.ds((h // 2) * 2 * head_dim, 2 * head_dim)
        q_ref = qe if h % 2 == 0 else qo
        s = lax.dot_general(
            k_ref[k0 : k0 + count, pair], q_ref[q0 : q0 + BLK, pair], NT, preferred_element_type=F32
        )
        s = table(s)
        top = jnp.max(s, axis=0, keepdims=True)
        p = jnp.exp(s - top)
        total = jnp.sum(p, axis=0, keepdims=True)
        mixed = jnp.dot(
            v_ref[h * head_dim : (h + 1) * head_dim, k0 : k0 + count],
            p.astype(BF16), preferred_element_type=F32,
        )
        return top, total, mixed

    span = rows + gcount

    def global_part(l):
        tops, totals, parts = [], [], []
        for h in range(heads):
            top, total, mixed = attend(h, ks, vt, 0, span, rows, lambda s: s + e_glob[...])
            tops.append(top)
            totals.append(total)
            parts.append(mixed)
        stats = three_parts(jnp.concatenate(tops, axis=0)) + three_parts(jnp.concatenate(totals, axis=0))
        pad = jnp.zeros((BLK - 6 * heads, BLK), F32)
        packed = jnp.transpose(jnp.concatenate(parts + list(stats) + [pad], axis=0))
        half = width // 2
        tail = packed[:, width:]
        upper = jnp.concatenate([packed[:, :half], tail], axis=1)
        lower = jnp.concatenate([packed[:, half:width], tail], axis=1)
        for o in range(owners):
            cut = slice(o * GROWS, (o + 1) * GROWS)
            rs_src[l, o] = jnp.concatenate([upper[cut], lower[cut]], axis=0).astype(BF16)
        others(owners, lambda peer: rs_copy(l, peer, me).start())

    def combine(l):
        rs_buf[l, me] = rs_src[l, me]
        others(n, lambda peer: rs_copy(l, me, peer).wait_recv())
        half = width // 2
        got = rs_buf[l].astype(F32)
        upper = got[:, :GROWS, :]
        lower = got[:, GROWS:, :]
        stats = upper[:, :, half:].reshape(n * GROWS, BLK).astype(BF16)
        top = jnp.dot(stats, expander(0), preferred_element_type=F32).reshape(n, GROWS, width)
        total = jnp.dot(stats, expander(24), preferred_element_type=F32).reshape(n, GROWS, width)
        value = jnp.concatenate([upper[:, :, :half], lower[:, :, :half]], axis=2)
        factor = jnp.exp(top - jnp.max(top, axis=0, keepdims=True))
        mix = jnp.sum(value * factor, axis=0) / jnp.sum(total * factor, axis=0)
        mix = jnp.concatenate([mix, mix], axis=0).astype(BF16)
        new = gown[...] + jnp.dot(mix, wout[l], preferred_element_type=F32)[:GROWS]
        gown[...] = new
        if l + 1 < LAYERS:
            new = norm_rows(new, gg_ref[l + 1 : l + 2, :])
        ag_buf[l, me] = fold(new).astype(BF16)
        others(n, lambda peer: ag_copy(l, peer, me).start())

    def gathered(l):
        others(owners, lambda peer: ag_copy(l, me, peer).wait_recv())
        got = ag_buf[l].astype(F32)
        half = width // 2
        return jnp.concatenate(
            [got[:, :GROWS].reshape(gcount, half), got[:, GROWS:].reshape(gcount, half)], axis=1
        ).astype(BF16)

    for l in range(LAYERS):
        if l == 0:
            for c in wcopies:
                c.wait()
            for w in range(LAYERS):
                wvt[w] = jnp.transpose(wqkv[w, :, 2 * width : 3 * width])
            project(0, 0, span)
        else:
            project(l, 0, rows)
            xa[l, rows:span, :] = gathered(l - 1)
            project(l, rows, gcount)

        global_part(l)

        for rb in range(2):
            for h in range(heads):
                b = bias_ref[l, h]

                def own_table(s):
                    return jnp.concatenate([s[:rows] + e_own[rb] * b, s[rows:]], axis=0)

                top, total, mixed = attend(h, ks, vt, 0, span, rb * BLK, own_table)
                m_a[rb, h : h + 1, :] = top
                l_a[rb, h : h + 1, :] = total
                o_a[rb, h * head_dim : (h + 1) * head_dim, :] = mixed

        wait_halo(l)
        if l == 0:
            @pl.when(has_left)
            def _():
                seg_to_right().wait_recv()

            @pl.when(has_right)
            def _():
                seg_to_left().wait_recv()

            r = lax.broadcasted_iota(jnp.int32, (BLK, BLK), 0)
            c = lax.broadcasted_iota(jnp.int32, (BLK, BLK), 1)
            for t in range(4):
                side, part = t // 2, t % 2
                column = down(seg_halo[side, part : part + 1, :])
                present = has_left if side == 0 else has_right
                absent = jnp.where(present, 0.0, NEG).astype(F32)
                for rb in range(2):
                    if not 0 <= t - rb < 3:
                        continue
                    row = jnp.broadcast_to(seg_own[rb : rb + 1, :], (BLK, BLK))
                    same = jnp.where(column == row, 1.0, 0.0).astype(F32)
                    if side == 0:
                        allowed = r + part * BLK >= c + rb * BLK
                    else:
                        allowed = r + part * BLK <= c + rb * BLK
                    e_halo[rb, (t - rb) * BLK : (t - rb + 1) * BLK, :] = (
                        jnp.where(allowed, same, NEG) + absent
                    )

        x = xh[l]
        kh[...] = jnp.dot(x, wqkv[l, :, width : 2 * width], preferred_element_type=F32).astype(BF16)
        vht[...] = lax.dot_general(wvt[l], x, NT, preferred_element_type=F32).astype(BF16)

        for rb in range(2):
            for h in range(heads):
                b = bias_ref[l, h]
                top_b, total_b, mixed_b = attend(
                    h, kh, vht, rb * BLK, 3 * BLK, rb * BLK, lambda s: s + e_halo[rb] * b
                )
                top_a = m_a[rb, h : h + 1, :]
                top = jnp.maximum(top_a, top_b)
                fa = jnp.exp(top_a - top)
                fb = jnp.exp(top_b - top)
                inv = 1.0 / (l_a[rb, h : h + 1, :] * fa + total_b * fb)
                mixt[h * head_dim : (h + 1) * head_dim, rb * BLK : (rb + 1) * BLK] = (
                    o_a[rb, h * head_dim : (h + 1) * head_dim, :] * (fa * inv) + mixed_b * (fb * inv)
                )
            if rb == 0:
                only_owner(functools.partial(combine, l))

        mix = jnp.transpose(mixt[...]).astype(BF16)
        new = stream[...] + jnp.dot(mix, wout[l], preferred_element_type=F32)
        if l + 1 < LAYERS:
            stream[...] = new
            xa[l + 1, 0:rows, :] = norm_rows(new, gl_ref[l + 1 : l + 2, :]).astype(BF16)
            send_halo(l + 1)
        else:
            out_ref[...] = new.astype(BF16)

    gout_ref[...] = gathered(LAYERS - 1)

    @pl.when(has_right)
    def _():
        seg_to_right().wait_send()
        for l in range(LAYERS):
            halo_to_right(l).wait_send()

    @pl.when(has_left)
    def _():
        seg_to_left().wait_send()
        for l in range(LAYERS):
            halo_to_left(l).wait_send()

    for l in range(LAYERS):
        others(owners, lambda peer: rs_copy(l, peer, me).wait_send())
        only_owner(lambda: others(n, lambda peer: ag_copy(l, peer, me).wait_send()))


def per_device(n, tokens, globals_in, seg_ids, table, w_qkv, w_out, gain_local, gain_global, seg_bias):
    rows, width = tokens.shape
    gcount = globals_in.shape[0]
    heads = seg_bias.shape[1]
    assert rows == 2 * BLK and gcount == BLK and heads == 8
    owners = min(n, gcount // GROWS)
    assert owners * GROWS == gcount
    span = rows + gcount
    vmem = pl.BlockSpec(memory_space=pltpu.VMEM)
    hbm = pl.BlockSpec(memory_space=pl.ANY)
    smem = pl.BlockSpec(memory_space=pltpu.SMEM)
    dma = pltpu.SemaphoreType.DMA
    V = pltpu.VMEM
    half = width // 2
    return pl.pallas_call(
        functools.partial(kernel, n, owners, heads),
        out_shape=(
            jax.ShapeDtypeStruct((rows, width), BF16),
            jax.ShapeDtypeStruct((gcount, width), BF16),
        ),
        in_specs=[vmem, vmem, vmem, vmem, hbm, hbm, vmem, vmem, smem],
        out_specs=(vmem, vmem),
        scratch_shapes=[
            V((LAYERS, width, 3 * width), BF16),
            V((LAYERS, width, width), BF16),
            V((LAYERS, width, width), BF16),
            V((LAYERS, span, width), BF16),
            V((LAYERS, 2 * rows, width), BF16),
            V((8, BLK), F32),
            V((2, 8, BLK), F32),
            V((span, width), BF16),
            V((span, width), BF16),
            V((span, width), BF16),
            V((width, span), BF16),
            V((2 * rows, width), BF16),
            V((width, 2 * rows), BF16),
            V((2, rows, BLK), F32),
            V((2, 3 * BLK, BLK), F32),
            V((span, BLK), F32),
            V((2, width, BLK), F32),
            V((2, heads, BLK), F32),
            V((2, heads, BLK), F32),
            V((width, rows), F32),
            V((rows, width), F32),
            V((gcount, width), F32),
            V((GROWS, width), F32),
            V((LAYERS, owners, 2 * GROWS, half + BLK), BF16),
            V((LAYERS, n, 2 * GROWS, half + BLK), BF16),
            V((LAYERS, owners, 2 * GROWS, half), BF16),
            dma((LAYERS + 1,)),
            dma((2,)),
            dma((2,)),
            dma((LAYERS, 2)),
            dma((LAYERS, 2)),
            dma((LAYERS, owners)),
            dma((LAYERS, n)),
            dma((LAYERS, n)),
            dma((LAYERS, owners)),
        ],
        compiler_params=pltpu.CompilerParams(
            collective_id=0, has_side_effects=True, vmem_limit_bytes=40 * 1024 * 1024
        ),
        name="encoder",
    )(
        tokens, globals_in, seg_ids.reshape(2, BLK), table.reshape(1, BLK),
        w_qkv, w_out, gain_local, gain_global, seg_bias,
    )


def solution(mesh):
    return jax.shard_map(
        functools.partial(per_device, mesh.shape["seq"]),
        mesh=mesh,
        in_specs=(
            P(("dp", "seq"), None),
            P("dp", None),
            P(("dp", "seq")),
            P("dp"),
            P(),
            P(),
            P(),
            P(),
            P(),
        ),
        out_specs=(P(("dp", "seq"), None), P("dp", None)),
        check_vma=False,
    )
```

time: 377 us -> 49.1 us (0.13)
  waiting for transfers between devices: 136 us -> 0 us
  blocking collectives: 128 us -> 0 us
  matrix products: 42.2 us -> 0 us
  Pallas kernels: 0 us -> 38.4 us
  local copies, waits for them, and re-layouts: 27.9 us -> 9.7 us
  starting transfers between devices: 14.7 us -> 0 us
  between operations: 14.7 us -> 0.66 us
  other arithmetic: 13.3 us -> 0 us
    psum x2 -> x0, waiting for transfers between devices: 136 us -> none  [per_device(): lax.psum((total * factor, weighted * factor[..., None]), 'seq')]
    pmax x2 -> x0, blocking collectives: 68.4 us -> none  [per_device(): top_all = lax.pmax(top, 'seq')]
    psum x2 -> x0, blocking collectives: 59.4 us -> none  [per_device(): lax.psum((total * factor, weighted * factor[..., None]), 'seq')]
    dot_general x24 -> x0, matrix products: 42.2 us -> none  [the longest x2 10.1 us: window_attend(): jnp.einsum('hts,shd->thd', probs.astype(jnp.bfloat16), values_ext, prefer...]
    pallas_call x0 -> x1, Pallas kernels: none -> 38.4 us  [per_device(): pl.pallas_call(functools.partial(kernel, n, owners, heads), out_shape=(ja...]
    slice x26 -> x0, local copies, waits for them, and re-layouts: 24.4 us -> none  [the longest x4 5.33 us: per_device(): values_ext = kv_ext[:, width:].reshape(-1, heads, head_dim)]
    ppermute x6 -> x0, starting transfers between devices: 14.6 us -> none  [the longest x3 10.8 us: with_halo(): lax.ppermute(lax.slice_in_dim(block, block.shape[dim] - width, None, axis...]
    reduce_sum x14 -> x0, other arithmetic: 9.08 us -> none  [the longest x4 5.24 us: window_attend(): total = jnp.sum(probs, axis=-1) + jnp.sum(gprobs, axis=-1)]
  transfers between devices with their start and end apart: 8 -> 0, of which waited for: 2 -> 0; matrix products, arithmetic and copies ran while one was open for 8% -> 0% of each run, Pallas kernels for 0% -> 0%
where the time goes in v1:
time: 49.1 us; the launch traced here: 48.8 us
  Pallas kernels  38.4 us (78%)
  local copies, waits for them, and re-layouts  9.7 us (20%)
  between operations  0.66 us (1%)
    pallas_call x1, Pallas kernels, per_device(): pl.pallas_call(functools.partial(kernel, n, owners, heads), out_shape=(ja...  38.4 us
    unnamed x20, local copies, waits for them, and re-layouts  9.7 us

profile of v1, /device:TPU:0, one launch (start us, length us, event | category | flops | bytes accessed | tf_op | source)
XLA Modules:
  0.0 48.8 jit_solution(16843464323045655227)
XLA Ops:
  0.6 0.0 copy-start
  0.6 1.9 %copy-done = bf16[2,512,1536]{2,1,0:T(8,128)(2,1)S(1)} copy-done((bf16[2,512,1536]{2,1,0:T(8,128)(2,1)S(1)}, bf16[2,512,1536]{2,1,0:T(8,128)(2,1)}, u32[]{:S(2)}) %copy-start) | copy-done | bytes 3145752
  2.5 0.0 copy-start.1
  2.5 1.2 %copy-done.1 = bf16[2,512,512]{2,1,0:T(8,128)(2,1)S(1)} copy-done((bf16[2,512,512]{2,1,0:T(8,128)(2,1)S(1)}, bf16[2,512,512]{2,1,0:T(8,128)(2,1)}, u32[]{:S(2)}) %copy-start.1) | copy-done | bytes 1048600
  3.7 0.0 copy-start.2
  3.8 0.9 %copy-done.2 = bf16[256,512]{1,0:T(8,128)(2,1)S(1)} copy-done((bf16[256,512]{1,0:T(8,128)(2,1)S(1)}, bf16[256,512]{1,0:T(8,128)(2,1)}, u32[]{:S(2)}) %copy-start.2) | copy-done | bytes 262168
  4.7 0.0 copy-start.3
  4.7 0.9 %copy-done.3 = bf16[128,512]{1,0:T(8,128)(2,1)S(1)} copy-done((bf16[128,512]{1,0:T(8,128)(2,1)S(1)}, bf16[128,512]{1,0:T(8,128)(2,1)}, u32[]{:S(2)}) %copy-start.3) | copy-done | bytes 131096
  5.6 0.0 copy-start.4
  5.6 0.7 %copy-done.4 = f32[2,512]{1,0:T(2,128)S(1)} copy-done((f32[2,512]{1,0:T(2,128)S(1)}, f32[2,512]{1,0:T(2,128)}, u32[]{:S(2)}) %copy-start.4) | copy-done | bytes 4120
  6.3 0.0 copy-start.5
  6.3 0.7 %copy-done.5 = f32[2,512]{1,0:T(2,128)S(1)} copy-done((f32[2,512]{1,0:T(2,128)S(1)}, f32[2,512]{1,0:T(2,128)}, u32[]{:S(2)}) %copy-start.5) | copy-done | bytes 4120
  7.0 0.0 copy-start.6
  7.0 0.7 %copy-done.6 = s32[256]{0:T(256)S(1)} copy-done((s32[256]{0:T(256)S(1)}, s32[256]{0:T(256)}, u32[]{:S(2)}) %copy-start.6) | copy-done | bytes 1048
  7.7 0.0 copy-start.7
  7.7 0.7 %copy-done.7 = f32[2,8]{1,0:T(2,128)S(1)} copy-done((f32[2,8]{1,0:T(2,128)S(1)}, f32[2,8]{1,0:T(2,128)}, u32[]{:S(2)}) %copy-start.7) | copy-done | bytes 88
  8.3 0.0 copy-start.8
  8.3 0.7 %copy-done.8 = s32[128]{0:T(128)S(1)} copy-done((s32[128]{0:T(128)S(1)}, s32[128]{0:T(128)}, u32[]{:S(2)}) %copy-start.8) | copy-done | bytes 536
  9.0 38.4 %encoder.1 = (bf16[256,512]{1,0:T(8,128)(2,1)S(1)}, bf16[128,512]{1,0:T(8,128)(2,1)S(1)}) custom-call(bf16[256,512]{1,0:T(8,128)(2,1)S(1)} %copy-done.2, bf16[128,512]{1,0:T(8,128)(2,1)S(1)} %copy-done.3, s32[2,128]{1,0:T(2,128)S(1)} %bitcast.2, s32[1,128]{1,0:T(1,128)S(1)} %bitcast.3, bf16[2,512,1536]{2,1,0:T(8,128)(2,1)S(1)} %copy-done, ...), custom_call_target="tpu_custom_call" | custom-call | tf_op jit(solution)/shard_map/encoder/pallas_call | solution.py:400
  47.4 0.7 %copy.13 = bf16[256,512]{1,0:T(8,128)(2,1)} copy(bf16[256,512]{1,0:T(8,128)(2,1)S(1)} %get-tuple-element.4) | data formatting | bytes 524288
  48.1 0.7 %copy.14 = bf16[128,512]{1,0:T(8,128)(2,1)} copy(bf16[128,512]{1,0:T(8,128)(2,1)S(1)} %get-tuple-element.5) | data formatting | bytes 262144
Async XLA Ops:
  0.6 1.9 %copy-start = (bf16[2,512,1536]{2,1,0:T(8,128)(2,1)S(1)}, bf16[2,512,1536]{2,1,0:T(8,128)(2,1)}, u32[]{:S(2)}) copy-start(bf16[2,512,1536]{2,1,0:T(8,128)(2,1)} %wqkv_hbm.1) | copy-start | bytes 9437188
  2.5 1.2 %copy-start.1 = (bf16[2,512,512]{2,1,0:T(8,128)(2,1)S(1)}, bf16[2,512,512]{2,1,0:T(8,128)(2,1)}, u32[]{:S(2)}) copy-start(bf16[2,512,512]{2,1,0:T(8,128)(2,1)} %wout_hbm.1) | copy-start | bytes 3145732
  3.7 0.9 %copy-start.2 = (bf16[256,512]{1,0:T(8,128)(2,1)S(1)}, bf16[256,512]{1,0:T(8,128)(2,1)}, u32[]{:S(2)}) copy-start(bf16[256,512]{1,0:T(8,128)(2,1)} %tok_ref.1) | copy-start | bytes 786436
  4.7 0.9 %copy-start.3 = (bf16[128,512]{1,0:T(8,128)(2,1)S(1)}, bf16[128,512]{1,0:T(8,128)(2,1)}, u32[]{:S(2)}) copy-start(bf16[128,512]{1,0:T(8,128)(2,1)} %glob_ref.1) | copy-start | bytes 393220
  5.6 0.7 %copy-start.4 = (f32[2,512]{1,0:T(2,128)S(1)}, f32[2,512]{1,0:T(2,128)}, u32[]{:S(2)}) copy-start(f32[2,512]{1,0:T(2,128)} %gl_ref.1) | copy-start | bytes 12292
  6.3 0.7 %copy-start.5 = (f32[2,512]{1,0:T(2,128)S(1)}, f32[2,512]{1,0:T(2,128)}, u32[]{:S(2)}) copy-start(f32[2,512]{1,0:T(2,128)} %gg_ref.1) | copy-start | bytes 12292
  7.0 0.7 %copy-start.6 = (s32[256]{0:T(256)S(1)}, s32[256]{0:T(256)}, u32[]{:S(2)}) copy-start(s32[256]{0:T(256)} %param.11) | copy-start | bytes 3076
  7.7 0.7 %copy-start.7 = (f32[2,8]{1,0:T(2,128)S(1)}, f32[2,8]{1,0:T(2,128)}, u32[]{:S(2)}) copy-start(f32[2,8]{1,0:T(2,128)} %bias_ref.1) | copy-start | bytes 196
  8.3 0.7 %copy-start.8 = (s32[128]{0:T(128)S(1)}, s32[128]{0:T(128)}, u32[]{:S(2)}) copy-start(s32[128]{0:T(128)} %param.12) | copy-start | bytes 1540

commit v2 on v1

--- a/solution.py
+++ b/solution.py
@@ -10,6 +10,8 @@
 LAYERS = 2
 BLK = 128
 GROWS = 8
+IDS = 64
+ONES = 16
 NEG = -1e30
 F32 = jnp.float32
 BF16 = jnp.bfloat16
@@ -37,12 +39,13 @@
 
 def kernel(
     n, owners, heads,
-    tok_ref, glob_ref, seg_ref, table_ref, wqkv_hbm, wout_hbm, gl_ref, gg_ref, bias_ref,
+    tok_hbm, glob_hbm, seg_hbm, table_hbm, wqkv_hbm, wout_hbm, gl_hbm, gg_hbm, bias_hbm,
     out_ref, gout_ref,
-    wqkv, wout, wvt, xa, xh, seg_own, seg_halo,
-    qe, qo, ks, vt, kh, vht, e_own, e_halo, e_glob,
-    o_a, m_a, l_a, mixt, stream, gstate, gown, rs_src, rs_buf, ag_buf,
-    w_sem, seg_send, seg_recv, h_send, h_recv, rs_send, rs_recv, ag_send, ag_recv,
+    tok_ref, glob_ref, seg_ref, table_ref, wqkv, wout, gl_ref, gg_ref, bias_ref,
+    wvt, xa, xh, seg_own, seg_halo,
+    qs, k_own, v_own, k_far, v_far, tri,
+    o_a, m_a, l_a, mixt, stream, gall, gown, rs_src, rs_buf, ag_buf,
+    in_sem, seg_send, seg_recv, h_send, h_recv, rs_send, rs_recv, ag_send, ag_recv,
 ):
     rows, width = tok_ref.shape
     gcount = glob_ref.shape[0]
@@ -62,13 +65,27 @@
             device_id_type=pl.DeviceIdType.MESH,
         )
 
-    wcopies = []
-    for l in range(LAYERS):
-        wcopies.append(pltpu.make_async_copy(wqkv_hbm.at[l], wqkv.at[l], w_sem.at[l]))
-    wcopies.append(pltpu.make_async_copy(wout_hbm, wout, w_sem.at[LAYERS]))
-    for c in wcopies:
-        c.start()
-
+    def load(i, src, dst):
+        copy = pltpu.make_async_copy(src, dst, in_sem.at[i])
+        copy.start()
+        return copy
+
+    tok_in = load(0, tok_hbm, tok_ref)
+    gl_in = load(1, gl_hbm, gl_ref)
+    seg_in = load(2, seg_hbm, seg_ref)
+    w_in = [load(3, wqkv_hbm.at[0], wqkv.at[0])]
+    small_in = [
+        load(4, glob_hbm, glob_ref),
+        load(5, table_hbm, table_ref),
+        load(6, gg_hbm, gg_ref),
+        load(7, bias_hbm, bias_ref),
+    ]
+    wout_in = load(8, wout_hbm, wout)
+    w_in += [load(8 + l, wqkv_hbm.at[l], wqkv.at[l]) for l in range(1, LAYERS)]
+
+    pairs = heads // 2
+    wide = 2 * BLK
+    seg_in.wait()
     seg_own[...] = jnp.zeros(seg_own.shape, F32)
     seg_own[0:2, :] = seg_ref[...].astype(F32)
 
@@ -84,6 +101,8 @@
         for l in range(LAYERS):
             xh[l, rows : 2 * rows, :] = jnp.zeros((rows, width), BF16)
 
+    tok_in.wait()
+    gl_in.wait()
     stream[...] = tok_ref[...].astype(F32)
     xa[0, 0:rows, :] = norm_rows(stream[...], gl_ref[0:1, :]).astype(BF16)
     pl.semaphore_wait(barrier, n - 1)
@@ -168,29 +187,62 @@
             ag_buf.at[l, source], ag_buf.at[l, source], ag_send.at[l, target], ag_recv.at[l, source], target
         )
 
-    gstate[...] = glob_ref[...].astype(F32)
+    for copy in small_in:
+        copy.wait()
+
+    xa[0, rows : rows + gcount, :] = norm_rows(glob_ref[...].astype(F32), gg_ref[0:1, :]).astype(BF16)
+    gall[...] = glob_ref[...].astype(F32)
 
     def take_own():
-        gown[...] = gstate[pl.ds(me * GROWS, GROWS), :]
+        gown[...] = gall[pl.ds(me * GROWS, GROWS), :]
 
     only_owner(take_own)
-    xa[0, rows : rows + gcount, :] = norm_rows(gstate[...], gg_ref[0:1, :]).astype(BF16)
+
+    lane = lax.broadcasted_iota(jnp.int32, (BLK, BLK), 1)
+    lane_id = lax.rem(lane, IDS)
+    lane_idf = lane_id.astype(F32)
+    low = lane < IDS
 
     def down(row):
         return jnp.transpose(jnp.broadcast_to(row, (BLK, BLK)))
 
-    for kb in range(2):
-        column = down(seg_own[kb : kb + 1, :])
-        for rb in range(2):
-            row = jnp.broadcast_to(seg_own[rb : rb + 1, :], (BLK, BLK))
-            e_own[rb, kb * BLK : (kb + 1) * BLK, :] = jnp.where(column == row, 1.0, 0.0).astype(F32)
-        trow = jnp.broadcast_to(table_ref[...].astype(F32), (BLK, BLK))
-        e_glob[kb * BLK : (kb + 1) * BLK, :] = jnp.where(column == trow, 0.0, NEG).astype(F32)
-    first = jnp.where(me == 0, 0.0, NEG).astype(F32)
-    e_glob[2 * BLK : 2 * BLK + gcount, :] = jnp.full((gcount, BLK), 0.0, F32) + first
-
-    lane = lax.broadcasted_iota(jnp.int32, (1, width), 1)
-    even = jnp.where(lax.rem(lane // head_dim, 2) == 0, 0.125, 0.0).astype(F32)
+    def marks(row):
+        return jnp.where(down(row) == lane_idf, 1.0, 0.0).astype(F32)
+
+    def put_marks(ref, at, value):
+        for p in range(pairs):
+            ref[at : at + BLK, p * wide + BLK : (p + 1) * wide] = value.astype(BF16)
+
+    outside = jnp.where(lane == 0, NEG, 0.0).astype(F32)
+    for rb in range(2):
+        own = marks(seg_own[rb : rb + 1, :])
+        put_marks(k_own, rb * BLK, own)
+        for l in range(LAYERS):
+            for h in range(heads):
+                b = jnp.broadcast_to(bias_ref[l : l + 1, h : h + 1], (BLK, BLK))
+                b_hi = b.astype(BF16).astype(F32)
+                qs[l, h // 2, rb, (h % 2) * BLK : (h % 2 + 1) * BLK, BLK:] = (
+                    own * jnp.where(low, b_hi, b - b_hi) + outside
+                ).astype(BF16)
+    hidden = jnp.where(me == 0, 0.0, 1.0).astype(F32)
+    g_marks = jnp.where(lane == IDS, 1.0, 0.0).astype(F32) * hidden
+    put_marks(k_own, rows, g_marks)
+    put_marks(k_far, rows, g_marks)
+    member = marks(table_ref[...].astype(F32))
+    g_side = jnp.where(low & (lane > 0), (1.0 - member) * NEG, 0.0) + jnp.where(lane == IDS, NEG, 0.0)
+    for l in range(LAYERS):
+        for h in range(heads):
+            qs[l, h // 2, 2, (h % 2) * BLK : (h % 2 + 1) * BLK, BLK:] = g_side.astype(BF16)
+
+    tr = lax.broadcasted_iota(jnp.int32, (BLK, wide), 0)
+    tc = lax.rem(lax.broadcasted_iota(jnp.int32, (BLK, wide), 1), BLK)
+    tri[0] = jnp.where(tr >= tc, 0.0, NEG).astype(F32)
+    tri[1] = jnp.where(tr <= tc, 0.0, NEG).astype(F32)
+    v_own[:, BLK:, :] = jnp.ones((pairs, ONES, rows + gcount), BF16)
+    v_far[:, BLK:, :] = jnp.ones((pairs, ONES, 2 * rows + gcount), BF16)
+
+    head_lane = lax.broadcasted_iota(jnp.int32, (1, BLK), 1)
+    even = jnp.where(head_lane < head_dim, 0.125, 0.0).astype(F32)
     odd = 0.125 - even
 
     pick = lax.broadcasted_iota(jnp.int32, (BLK, width), 0)
@@ -200,43 +252,58 @@
         hit = (pick == base + head_of) | (pick == base + 8 + head_of) | (pick == base + 16 + head_of)
         return jnp.where(hit, 1.0, 0.0).astype(F32).astype(BF16)
 
-    def project(l, lo, count):
-        x = xa[l, lo : lo + count, :]
+    def put_keys(l, x, *places):
+        count = x.shape[0]
+        k = jnp.dot(x, wqkv[l, :, width : 2 * width], preferred_element_type=F32).astype(BF16)
+        v = lax.dot_general(wvt[l], x, NT, preferred_element_type=F32).astype(BF16)
+        for k_ref, v_ref, at in places:
+            for p in range(pairs):
+                k_ref[at : at + count, p * wide : p * wide + BLK] = k[:, p * BLK : (p + 1) * BLK]
+                v_ref[p, 0:BLK, at : at + count] = v[p * BLK : (p + 1) * BLK]
+
+    def put_queries(l, x, first):
         q = jnp.dot(x, wqkv[l, :, 0:width], preferred_element_type=F32)
-        qe[lo : lo + count, :] = (q * even).astype(BF16)
-        qo[lo : lo + count, :] = (q * odd).astype(BF16)
-        ks[lo : lo + count, :] = jnp.dot(
-            x, wqkv[l, :, width : 2 * width], preferred_element_type=F32
-        ).astype(BF16)
-        vt[:, lo : lo + count] = lax.dot_general(
-            wvt[l], x, NT, preferred_element_type=F32
-        ).astype(BF16)
-
-    def attend(h, k_ref, v_ref, k0, count, q0, table):
-        pair = pl.ds((h // 2) * 2 * head_dim, 2 * head_dim)
-        q_ref = qe if h % 2 == 0 else qo
+        for b in range(x.shape[0] // BLK):
+            for p in range(pairs):
+                part = q[b * BLK : (b + 1) * BLK, p * BLK : (p + 1) * BLK]
+                qs[l, p, first + b, 0:BLK, 0:BLK] = (part * even).astype(BF16)
+                qs[l, p, first + b, BLK:, 0:BLK] = (part * odd).astype(BF16)
+
+    def project_local(l):
+        x = xa[l, 0:rows, :]
+        put_queries(l, x, 0)
+        put_keys(l, x, (k_own, v_own, 0))
+
+    def project_global(l):
+        x = xa[l, rows : rows + gcount, :]
+        put_queries(l, x, 2)
+        put_keys(l, x, (k_own, v_own, rows), (k_far, v_far, rows))
+
+    def attend(l, p, rb, k_ref, v_ref, k0, count, masked=False):
         s = lax.dot_general(
-            k_ref[k0 : k0 + count, pair], q_ref[q0 : q0 + BLK, pair], NT, preferred_element_type=F32
-        )
-        s = table(s)
+            k_ref[k0 : k0 + count, p * wide : (p + 1) * wide], qs[l, p, rb], NT,
+            preferred_element_type=F32,
+        )
+        if masked:
+            s = jnp.concatenate(
+                [s[:BLK] + tri[0], s[BLK : count - BLK], s[count - BLK :] + tri[1]], axis=0
+            )
         top = jnp.max(s, axis=0, keepdims=True)
-        p = jnp.exp(s - top)
-        total = jnp.sum(p, axis=0, keepdims=True)
-        mixed = jnp.dot(
-            v_ref[h * head_dim : (h + 1) * head_dim, k0 : k0 + count],
-            p.astype(BF16), preferred_element_type=F32,
-        )
-        return top, total, mixed
+        probs = jnp.exp(s - top).astype(BF16)
+        mixed = jnp.dot(v_ref[p, :, k0 : k0 + count], probs, preferred_element_type=F32)
+        value = jnp.concatenate([mixed[:head_dim, :BLK], mixed[head_dim:BLK, BLK:]], axis=1)
+        return top, mixed[BLK : BLK + 1], value
 
     span = rows + gcount
 
     def global_part(l):
         tops, totals, parts = [], [], []
-        for h in range(heads):
-            top, total, mixed = attend(h, ks, vt, 0, span, rows, lambda s: s + e_glob[...])
-            tops.append(top)
-            totals.append(total)
-            parts.append(mixed)
+        for p in range(pairs):
+            top, total, value = attend(l, p, 2, k_own, v_own, 0, span)
+            for lanes in (slice(0, BLK), slice(BLK, wide)):
+                tops.append(top[:, lanes])
+                totals.append(total[:, lanes])
+                parts.append(value[:, lanes])
         stats = three_parts(jnp.concatenate(tops, axis=0)) + three_parts(jnp.concatenate(totals, axis=0))
         pad = jnp.zeros((BLK - 6 * heads, BLK), F32)
         packed = jnp.transpose(jnp.concatenate(parts + list(stats) + [pad], axis=0))
@@ -278,31 +345,34 @@
             [got[:, :GROWS].reshape(gcount, half), got[:, GROWS:].reshape(gcount, half)], axis=1
         ).astype(BF16)
 
+    def near_part(l):
+        for rb in range(2):
+            for p in range(pairs):
+                top, total, value = attend(l, p, rb, k_own, v_own, 0, rows)
+                m_a[rb, p] = top
+                l_a[rb, p] = total
+                o_a[rb, p] = value
+
+    def turn(l):
+        w_in[l].wait()
+        wvt[l] = jnp.transpose(wqkv[l, :, 2 * width : 3 * width])
+
     for l in range(LAYERS):
         if l == 0:
-            for c in wcopies:
-                c.wait()
-            for w in range(LAYERS):
-                wvt[w] = jnp.transpose(wqkv[w, :, 2 * width : 3 * width])
-            project(0, 0, span)
+            turn(0)
+            project_global(0)
+            project_local(0)
+            global_part(0)
+            near_part(0)
+            wout_in.wait()
+            for w in range(1, LAYERS):
+                turn(w)
         else:
-            project(l, 0, rows)
+            project_local(l)
+            near_part(l)
             xa[l, rows:span, :] = gathered(l - 1)
-            project(l, rows, gcount)
-
-        global_part(l)
-
-        for rb in range(2):
-            for h in range(heads):
-                b = bias_ref[l, h]
-
-                def own_table(s):
-                    return jnp.concatenate([s[:rows] + e_own[rb] * b, s[rows:]], axis=0)
-
-                top, total, mixed = attend(h, ks, vt, 0, span, rb * BLK, own_table)
-                m_a[rb, h : h + 1, :] = top
-                l_a[rb, h : h + 1, :] = total
-                o_a[rb, h * head_dim : (h + 1) * head_dim, :] = mixed
+            project_global(l)
+            global_part(l)
 
         wait_halo(l)
         if l == 0:
@@ -314,46 +384,30 @@
             def _():
                 seg_to_left().wait_recv()
 
-            r = lax.broadcasted_iota(jnp.int32, (BLK, BLK), 0)
-            c = lax.broadcasted_iota(jnp.int32, (BLK, BLK), 1)
-            for t in range(4):
-                side, part = t // 2, t % 2
-                column = down(seg_halo[side, part : part + 1, :])
-                present = has_left if side == 0 else has_right
-                absent = jnp.where(present, 0.0, NEG).astype(F32)
-                for rb in range(2):
-                    if not 0 <= t - rb < 3:
-                        continue
-                    row = jnp.broadcast_to(seg_own[rb : rb + 1, :], (BLK, BLK))
-                    same = jnp.where(column == row, 1.0, 0.0).astype(F32)
-                    if side == 0:
-                        allowed = r + part * BLK >= c + rb * BLK
-                    else:
-                        allowed = r + part * BLK <= c + rb * BLK
-                    e_halo[rb, (t - rb) * BLK : (t - rb + 1) * BLK, :] = (
-                        jnp.where(allowed, same, NEG) + absent
+            for side in range(2):
+                for part in range(2):
+                    put_marks(
+                        k_far, side * span + part * BLK, marks(seg_halo[side, part : part + 1, :])
                     )
 
-        x = xh[l]
-        kh[...] = jnp.dot(x, wqkv[l, :, width : 2 * width], preferred_element_type=F32).astype(BF16)
-        vht[...] = lax.dot_general(wvt[l], x, NT, preferred_element_type=F32).astype(BF16)
+        put_keys(l, xh[l, 0:rows, :], (k_far, v_far, 0))
+        put_keys(l, xh[l, rows : 2 * rows, :], (k_far, v_far, span))
+        only_owner(functools.partial(combine, l))
 
         for rb in range(2):
-            for h in range(heads):
-                b = bias_ref[l, h]
-                top_b, total_b, mixed_b = attend(
-                    h, kh, vht, rb * BLK, 3 * BLK, rb * BLK, lambda s: s + e_halo[rb] * b
+            for p in range(pairs):
+                top_b, total_b, value_b = attend(
+                    l, p, rb, k_far, v_far, rb * BLK, 4 * BLK, masked=True
                 )
-                top_a = m_a[rb, h : h + 1, :]
+                top_a = m_a[rb, p]
                 top = jnp.maximum(top_a, top_b)
                 fa = jnp.exp(top_a - top)
                 fb = jnp.exp(top_b - top)
-                inv = 1.0 / (l_a[rb, h : h + 1, :] * fa + total_b * fb)
-                mixt[h * head_dim : (h + 1) * head_dim, rb * BLK : (rb + 1) * BLK] = (
-                    o_a[rb, h * head_dim : (h + 1) * head_dim, :] * (fa * inv) + mixed_b * (fb * inv)
-                )
-            if rb == 0:
-                only_owner(functools.partial(combine, l))
+                inv = 1.0 / (l_a[rb, p] * fa + total_b * fb)
+                value = o_a[rb, p] * (fa * inv) + value_b * (fb * inv)
+                lanes = slice(rb * BLK, (rb + 1) * BLK)
+                mixt[p * BLK : p * BLK + head_dim, lanes] = value[:, :BLK]
+                mixt[p * BLK + head_dim : (p + 1) * BLK, lanes] = value[:, BLK:]
 
         mix = jnp.transpose(mixt[...]).astype(BF16)
         new = stream[...] + jnp.dot(mix, wout[l], preferred_element_type=F32)
@@ -392,39 +446,44 @@
     assert owners * GROWS == gcount
     span = rows + gcount
     vmem = pl.BlockSpec(memory_space=pltpu.VMEM)
-    hbm = pl.BlockSpec(memory_space=pl.ANY)
-    smem = pl.BlockSpec(memory_space=pltpu.SMEM)
+    hbm = pl.BlockSpec(memory_space=pltpu.HBM)
     dma = pltpu.SemaphoreType.DMA
     V = pltpu.VMEM
     half = width // 2
+    pairs, wide, head_dim = heads // 2, 2 * BLK, width // heads
+    assert 2 * head_dim == BLK
     return pl.pallas_call(
         functools.partial(kernel, n, owners, heads),
         out_shape=(
             jax.ShapeDtypeStruct((rows, width), BF16),
             jax.ShapeDtypeStruct((gcount, width), BF16),
         ),
-        in_specs=[vmem, vmem, vmem, vmem, hbm, hbm, vmem, vmem, smem],
+        in_specs=[hbm] * 9,
         out_specs=(vmem, vmem),
         scratch_shapes=[
+            V((rows, width), BF16),
+            V((gcount, width), BF16),
+            V((2, BLK), jnp.int32),
+            V((1, BLK), jnp.int32),
             V((LAYERS, width, 3 * width), BF16),
             V((LAYERS, width, width), BF16),
+            V((LAYERS, width), F32),
+            V((LAYERS, width), F32),
+            V((LAYERS, heads), F32),
             V((LAYERS, width, width), BF16),
             V((LAYERS, span, width), BF16),
             V((LAYERS, 2 * rows, width), BF16),
             V((8, BLK), F32),
             V((2, 8, BLK), F32),
-            V((span, width), BF16),
-            V((span, width), BF16),
-            V((span, width), BF16),
-            V((width, span), BF16),
-            V((2 * rows, width), BF16),
-            V((width, 2 * rows), BF16),
-            V((2, rows, BLK), F32),
-            V((2, 3 * BLK, BLK), F32),
-            V((span, BLK), F32),
-            V((2, width, BLK), F32),
-            V((2, heads, BLK), F32),
-            V((2, heads, BLK), F32),
+            V((LAYERS, pairs, 3, wide, wide), BF16),
+            V((span, pairs * wide), BF16),
+            V((pairs, BLK + ONES, span), BF16),
+            V((2 * rows + gcount, pairs * wide), BF16),
+            V((pairs, BLK + ONES, 2 * rows + gcount), BF16),
+            V((2, BLK, wide), F32),
+            V((2, pairs, head_dim, wide), F32),
+            V((2, pairs, 1, wide), F32),
+            V((2, pairs, 1, wide), F32),
             V((width, rows), F32),
             V((rows, width), F32),
             V((gcount, width), F32),
@@ -432,7 +491,7 @@
             V((LAYERS, owners, 2 * GROWS, half + BLK), BF16),
             V((LAYERS, n, 2 * GROWS, half + BLK), BF16),
             V((LAYERS, owners, 2 * GROWS, half), BF16),
-            dma((LAYERS + 1,)),
+            dma((8 + LAYERS,)),
             dma((2,)),
             dma((2,)),
             dma((LAYERS, 2)),

time: 49.1 us -> 47.7 us (0.971)
  Pallas kernels: 38.4 us -> 37 us
    pallas_call x1, Pallas kernels: 38.4 us -> 37 us  [per_device(): pl.pallas_call(functools.partial(kernel, n, owners, heads), out_shape=(ja...]
where the time goes in v2:
time: 47.7 us; the launch traced here: 47.4 us
  Pallas kernels  37 us (78%)
  local copies, waits for them, and re-layouts  9.7 us (20%)
  between operations  0.66 us (1%)
    pallas_call x1, Pallas kernels, per_device(): pl.pallas_call(functools.partial(kernel, n, owners, heads), out_shape=(ja...  37 us
    unnamed x20, local copies, waits for them, and re-layouts  9.7 us

profile of v2, /device:TPU:0, one launch (start us, length us, event | category | flops | bytes accessed | tf_op | source)
XLA Modules:
  0.0 47.4 jit_solution(3522863259219233664)
XLA Ops:
  0.6 0.0 copy-start
  0.6 1.9 %copy-done = bf16[2,512,1536]{2,1,0:T(8,128)(2,1)S(1)} copy-done((bf16[2,512,1536]{2,1,0:T(8,128)(2,1)S(1)}, bf16[2,512,1536]{2,1,0:T(8,128)(2,1)}, u32[]{:S(2)}) %copy-start) | copy-done | bytes 3145752
  2.5 0.0 copy-start.1
  2.5 1.2 %copy-done.1 = bf16[2,512,512]{2,1,0:T(8,128)(2,1)S(1)} copy-done((bf16[2,512,512]{2,1,0:T(8,128)(2,1)S(1)}, bf16[2,512,512]{2,1,0:T(8,128)(2,1)}, u32[]{:S(2)}) %copy-start.1) | copy-done | bytes 1048600
  3.7 0.0 copy-start.2
  3.8 0.9 %copy-done.2 = bf16[256,512]{1,0:T(8,128)(2,1)S(1)} copy-done((bf16[256,512]{1,0:T(8,128)(2,1)S(1)}, bf16[256,512]{1,0:T(8,128)(2,1)}, u32[]{:S(2)}) %copy-start.2) | copy-done | bytes 262168
  4.7 0.0 copy-start.3
  4.7 0.9 %copy-done.3 = bf16[128,512]{1,0:T(8,128)(2,1)S(1)} copy-done((bf16[128,512]{1,0:T(8,128)(2,1)S(1)}, bf16[128,512]{1,0:T(8,128)(2,1)}, u32[]{:S(2)}) %copy-start.3) | copy-done | bytes 131096
  5.6 0.0 copy-start.4
  5.6 0.7 %copy-done.4 = f32[2,512]{1,0:T(2,128)S(1)} copy-done((f32[2,512]{1,0:T(2,128)S(1)}, f32[2,512]{1,0:T(2,128)}, u32[]{:S(2)}) %copy-start.4) | copy-done | bytes 4120
  6.3 0.0 copy-start.5
  6.3 0.7 %copy-done.5 = f32[2,512]{1,0:T(2,128)S(1)} copy-done((f32[2,512]{1,0:T(2,128)S(1)}, f32[2,512]{1,0:T(2,128)}, u32[]{:S(2)}) %copy-start.5) | copy-done | bytes 4120
  7.0 0.0 copy-start.6
  7.0 0.7 %copy-done.6 = s32[256]{0:T(256)S(1)} copy-done((s32[256]{0:T(256)S(1)}, s32[256]{0:T(256)}, u32[]{:S(2)}) %copy-start.6) | copy-done | bytes 1048
  7.7 0.0 copy-start.7
  7.7 0.7 %copy-done.7 = f32[2,8]{1,0:T(2,128)S(1)} copy-done((f32[2,8]{1,0:T(2,128)S(1)}, f32[2,8]{1,0:T(2,128)}, u32[]{:S(2)}) %copy-start.7) | copy-done | bytes 88
  8.3 0.0 copy-start.8
  8.3 0.7 %copy-done.8 = s32[128]{0:T(128)S(1)} copy-done((s32[128]{0:T(128)S(1)}, s32[128]{0:T(128)}, u32[]{:S(2)}) %copy-start.8) | copy-done | bytes 536
  9.0 37.0 %encoder.1 = (bf16[256,512]{1,0:T(8,128)(2,1)S(1)}, bf16[128,512]{1,0:T(8,128)(2,1)S(1)}) custom-call(bf16[256,512]{1,0:T(8,128)(2,1)S(1)} %copy-done.2, bf16[128,512]{1,0:T(8,128)(2,1)S(1)} %copy-done.3, s32[2,128]{1,0:T(2,128)S(1)} %bitcast.2, s32[1,128]{1,0:T(1,128)S(1)} %bitcast.3, bf16[2,512,1536]{2,1,0:T(8,128)(2,1)S(1)} %copy-done, ...), custom_call_target="tpu_custom_call" | custom-call | tf_op jit(solution)/shard_map/encoder/pallas_call | solution.py:455
  46.0 0.7 %copy.13 = bf16[256,512]{1,0:T(8,128)(2,1)} copy(bf16[256,512]{1,0:T(8,128)(2,1)S(1)} %get-tuple-element.4) | data formatting | bytes 524288
  46.7 0.7 %copy.14 = bf16[128,512]{1,0:T(8,128)(2,1)} copy(bf16[128,512]{1,0:T(8,128)(2,1)S(1)} %get-tuple-element.5) | data formatting | bytes 262144
Async XLA Ops:
  0.6 1.9 %copy-start = (bf16[2,512,1536]{2,1,0:T(8,128)(2,1)S(1)}, bf16[2,512,1536]{2,1,0:T(8,128)(2,1)}, u32[]{:S(2)}) copy-start(bf16[2,512,1536]{2,1,0:T(8,128)(2,1)} %wqkv_hbm.1) | copy-start | bytes 9437188
  2.5 1.2 %copy-start.1 = (bf16[2,512,512]{2,1,0:T(8,128)(2,1)S(1)}, bf16[2,512,512]{2,1,0:T(8,128)(2,1)}, u32[]{:S(2)}) copy-start(bf16[2,512,512]{2,1,0:T(8,128)(2,1)} %wout_hbm.1) | copy-start | bytes 3145732
  3.7 0.9 %copy-start.2 = (bf16[256,512]{1,0:T(8,128)(2,1)S(1)}, bf16[256,512]{1,0:T(8,128)(2,1)}, u32[]{:S(2)}) copy-start(bf16[256,512]{1,0:T(8,128)(2,1)} %tok_hbm.1) | copy-start | bytes 786436
  4.7 0.9 %copy-start.3 = (bf16[128,512]{1,0:T(8,128)(2,1)S(1)}, bf16[128,512]{1,0:T(8,128)(2,1)}, u32[]{:S(2)}) copy-start(bf16[128,512]{1,0:T(8,128)(2,1)} %glob_hbm.1) | copy-start | bytes 393220
  5.6 0.7 %copy-start.4 = (f32[2,512]{1,0:T(2,128)S(1)}, f32[2,512]{1,0:T(2,128)}, u32[]{:S(2)}) copy-start(f32[2,512]{1,0:T(2,128)} %gl_hbm.1) | copy-start | bytes 12292
  6.3 0.7 %copy-start.5 = (f32[2,512]{1,0:T(2,128)S(1)}, f32[2,512]{1,0:T(2,128)}, u32[]{:S(2)}) copy-start(f32[2,512]{1,0:T(2,128)} %gg_hbm.1) | copy-start | bytes 12292
  7.0 0.7 %copy-start.6 = (s32[256]{0:T(256)S(1)}, s32[256]{0:T(256)}, u32[]{:S(2)}) copy-start(s32[256]{0:T(256)} %param.11) | copy-start | bytes 3076
  7.7 0.7 %copy-start.7 = (f32[2,8]{1,0:T(2,128)S(1)}, f32[2,8]{1,0:T(2,128)}, u32[]{:S(2)}) copy-start(f32[2,8]{1,0:T(2,128)} %bias_hbm.1) | copy-start | bytes 196
  8.3 0.7 %copy-start.8 = (s32[128]{0:T(128)S(1)}, s32[128]{0:T(128)}, u32[]{:S(2)}) copy-start(s32[128]{0:T(128)} %param.12) | copy-start | bytes 1540

commit v3 on v2

--- a/solution.py
+++ b/solution.py
@@ -12,10 +12,10 @@
 GROWS = 8
 IDS = 64
 ONES = 16
+VMEM_BYTES = 62 * 1024 * 1024
 NEG = -1e30
 F32 = jnp.float32
 BF16 = jnp.bfloat16
-NT = (((1,), (1,)), ((), ()))
 
 
 def norm_rows(values, gain):
@@ -42,8 +42,8 @@
     tok_hbm, glob_hbm, seg_hbm, table_hbm, wqkv_hbm, wout_hbm, gl_hbm, gg_hbm, bias_hbm,
     out_ref, gout_ref,
     tok_ref, glob_ref, seg_ref, table_ref, wqkv, wout, gl_ref, gg_ref, bias_ref,
-    wvt, xa, xh, seg_own, seg_halo,
-    qs, k_own, v_own, k_far, v_far, tri,
+    xa, xh, seg_own, seg_halo,
+    qs, k_own, v_own, k_far, v_far, tri, spread,
     o_a, m_a, l_a, mixt, stream, gall, gown, rs_src, rs_buf, ag_buf,
     in_sem, seg_send, seg_recv, h_send, h_recv, rs_send, rs_recv, ag_send, ag_recv,
 ):
@@ -199,9 +199,10 @@
     only_owner(take_own)
 
     lane = lax.broadcasted_iota(jnp.int32, (BLK, BLK), 1)
-    lane_id = lax.rem(lane, IDS)
-    lane_idf = lane_id.astype(F32)
-    low = lane < IDS
+    lane_idf = (lane & (IDS - 1)).astype(F32)
+    deep = lax.broadcasted_iota(jnp.int32, (BLK, BLK), 0)
+    deep_idf = (deep & (IDS - 1)).astype(F32)
+    low = deep < IDS
 
     def down(row):
         return jnp.transpose(jnp.broadcast_to(row, (BLK, BLK)))
@@ -213,49 +214,55 @@
         for p in range(pairs):
             ref[at : at + BLK, p * wide + BLK : (p + 1) * wide] = value.astype(BF16)
 
-    outside = jnp.where(lane == 0, NEG, 0.0).astype(F32)
+    for l in range(LAYERS):
+        for p in range(pairs):
+            for b in range(3):
+                qs[l, p, b, 0:BLK, :] = jnp.zeros((BLK, wide), BF16)
+
+    outside = jnp.where(deep == 0, NEG, 0.0).astype(F32)
     for rb in range(2):
-        own = marks(seg_own[rb : rb + 1, :])
-        put_marks(k_own, rb * BLK, own)
+        row = seg_own[rb : rb + 1, :]
+        put_marks(k_own, rb * BLK, marks(row))
+        own = jnp.where(jnp.broadcast_to(row, (BLK, BLK)) == deep_idf, 1.0, 0.0).astype(F32)
         for l in range(LAYERS):
             for h in range(heads):
                 b = jnp.broadcast_to(bias_ref[l : l + 1, h : h + 1], (BLK, BLK))
                 b_hi = b.astype(BF16).astype(F32)
-                qs[l, h // 2, rb, (h % 2) * BLK : (h % 2 + 1) * BLK, BLK:] = (
+                qs[l, h // 2, rb, BLK:, (h % 2) * BLK : (h % 2 + 1) * BLK] = (
                     own * jnp.where(low, b_hi, b - b_hi) + outside
                 ).astype(BF16)
     hidden = jnp.where(me == 0, 0.0, 1.0).astype(F32)
     g_marks = jnp.where(lane == IDS, 1.0, 0.0).astype(F32) * hidden
     put_marks(k_own, rows, g_marks)
     put_marks(k_far, rows, g_marks)
-    member = marks(table_ref[...].astype(F32))
-    g_side = jnp.where(low & (lane > 0), (1.0 - member) * NEG, 0.0) + jnp.where(lane == IDS, NEG, 0.0)
+    member = jnp.broadcast_to(table_ref[...].astype(F32), (BLK, BLK)) == deep_idf
+    g_side = jnp.where((low & (deep > 0) & jnp.logical_not(member)) | (deep == IDS), NEG, 0.0)
+    g_side = g_side.astype(F32).astype(BF16)
     for l in range(LAYERS):
-        for h in range(heads):
-            qs[l, h // 2, 2, (h % 2) * BLK : (h % 2 + 1) * BLK, BLK:] = g_side.astype(BF16)
+        for p in range(pairs):
+            qs[l, p, 2, BLK:, 0:BLK] = g_side
+            qs[l, p, 2, BLK:, BLK:] = g_side
 
     tr = lax.broadcasted_iota(jnp.int32, (BLK, wide), 0)
-    tc = lax.rem(lax.broadcasted_iota(jnp.int32, (BLK, wide), 1), BLK)
+    tc = lax.broadcasted_iota(jnp.int32, (BLK, wide), 1) & (BLK - 1)
     tri[0] = jnp.where(tr >= tc, 0.0, NEG).astype(F32)
     tri[1] = jnp.where(tr <= tc, 0.0, NEG).astype(F32)
     v_own[:, BLK:, :] = jnp.ones((pairs, ONES, rows + gcount), BF16)
     v_far[:, BLK:, :] = jnp.ones((pairs, ONES, 2 * rows + gcount), BF16)
 
-    head_lane = lax.broadcasted_iota(jnp.int32, (1, BLK), 1)
-    even = jnp.where(head_lane < head_dim, 0.125, 0.0).astype(F32)
-    odd = 0.125 - even
-
     pick = lax.broadcasted_iota(jnp.int32, (BLK, width), 0)
-    head_of = lax.broadcasted_iota(jnp.int32, (BLK, width), 1) // head_dim
-
-    def expander(base):
-        hit = (pick == base + head_of) | (pick == base + 8 + head_of) | (pick == base + 16 + head_of)
-        return jnp.where(hit, 1.0, 0.0).astype(F32).astype(BF16)
+    start = lax.broadcasted_iota(jnp.int32, (BLK, width), 1) & (head_dim - 1)
+    head_of = (lax.broadcasted_iota(jnp.int32, (BLK, width), 1) - start).astype(F32) * (1.0 / head_dim)
+    pick_head = (pick & 7).astype(F32)
+    for i in range(2):
+        hit = (pick_head == head_of) & (pick >= 24 * i) & (pick < 24 * (i + 1))
+        spread[i] = jnp.where(hit, 1.0, 0.0).astype(F32).astype(BF16)
 
     def put_keys(l, x, *places):
         count = x.shape[0]
         k = jnp.dot(x, wqkv[l, :, width : 2 * width], preferred_element_type=F32).astype(BF16)
-        v = lax.dot_general(wvt[l], x, NT, preferred_element_type=F32).astype(BF16)
+        v = jnp.dot(x, wqkv[l, :, 2 * width : 3 * width], preferred_element_type=F32).astype(BF16)
+        v = jnp.transpose(v)
         for k_ref, v_ref, at in places:
             for p in range(pairs):
                 k_ref[at : at + count, p * wide : p * wide + BLK] = k[:, p * BLK : (p + 1) * BLK]
@@ -263,11 +270,13 @@
 
     def put_queries(l, x, first):
         q = jnp.dot(x, wqkv[l, :, 0:width], preferred_element_type=F32)
+        q = jnp.transpose((q * 0.125).astype(BF16))
         for b in range(x.shape[0] // BLK):
             for p in range(pairs):
-                part = q[b * BLK : (b + 1) * BLK, p * BLK : (p + 1) * BLK]
-                qs[l, p, first + b, 0:BLK, 0:BLK] = (part * even).astype(BF16)
-                qs[l, p, first + b, BLK:, 0:BLK] = (part * odd).astype(BF16)
+                lanes = slice(b * BLK, (b + 1) * BLK)
+                at = p * BLK
+                qs[l, p, first + b, 0:head_dim, 0:BLK] = q[at : at + head_dim, lanes]
+                qs[l, p, first + b, head_dim:BLK, BLK:] = q[at + head_dim : at + BLK, lanes]
 
     def project_local(l):
         x = xa[l, 0:rows, :]
@@ -280,8 +289,8 @@
         put_keys(l, x, (k_own, v_own, rows), (k_far, v_far, rows))
 
     def attend(l, p, rb, k_ref, v_ref, k0, count, masked=False):
-        s = lax.dot_general(
-            k_ref[k0 : k0 + count, p * wide : (p + 1) * wide], qs[l, p, rb], NT,
+        s = jnp.dot(
+            k_ref[k0 : k0 + count, p * wide : (p + 1) * wide], qs[l, p, rb],
             preferred_element_type=F32,
         )
         if masked:
@@ -324,8 +333,8 @@
         upper = got[:, :GROWS, :]
         lower = got[:, GROWS:, :]
         stats = upper[:, :, half:].reshape(n * GROWS, BLK).astype(BF16)
-        top = jnp.dot(stats, expander(0), preferred_element_type=F32).reshape(n, GROWS, width)
-        total = jnp.dot(stats, expander(24), preferred_element_type=F32).reshape(n, GROWS, width)
+        top = jnp.dot(stats, spread[0], preferred_element_type=F32).reshape(n, GROWS, width)
+        total = jnp.dot(stats, spread[1], preferred_element_type=F32).reshape(n, GROWS, width)
         value = jnp.concatenate([upper[:, :, :half], lower[:, :, :half]], axis=2)
         factor = jnp.exp(top - jnp.max(top, axis=0, keepdims=True))
         mix = jnp.sum(value * factor, axis=0) / jnp.sum(total * factor, axis=0)
@@ -353,21 +362,16 @@
                 l_a[rb, p] = total
                 o_a[rb, p] = value
 
-    def turn(l):
-        w_in[l].wait()
-        wvt[l] = jnp.transpose(wqkv[l, :, 2 * width : 3 * width])
-
     for l in range(LAYERS):
         if l == 0:
-            turn(0)
+            w_in[0].wait()
             project_global(0)
             project_local(0)
             global_part(0)
             near_part(0)
             wout_in.wait()
-            for w in range(1, LAYERS):
-                turn(w)
         else:
+            w_in[l].wait()
             project_local(l)
             near_part(l)
             xa[l, rows:span, :] = gathered(l - 1)
@@ -470,7 +474,6 @@
             V((LAYERS, width), F32),
             V((LAYERS, width), F32),
             V((LAYERS, heads), F32),
-            V((LAYERS, width, width), BF16),
             V((LAYERS, span, width), BF16),
             V((LAYERS, 2 * rows, width), BF16),
             V((8, BLK), F32),
@@ -481,6 +484,7 @@
             V((2 * rows + gcount, pairs * wide), BF16),
             V((pairs, BLK + ONES, 2 * rows + gcount), BF16),
             V((2, BLK, wide), F32),
+            V((2, BLK, width), BF16),
             V((2, pairs, head_dim, wide), F32),
             V((2, pairs, 1, wide), F32),
             V((2, pairs, 1, wide), F32),
@@ -502,7 +506,7 @@
             dma((LAYERS, owners)),
         ],
         compiler_params=pltpu.CompilerParams(
-            collective_id=0, has_side_effects=True, vmem_limit_bytes=40 * 1024 * 1024
+            collective_id=0, has_side_effects=True, vmem_limit_bytes=VMEM_BYTES
         ),
         name="encoder",
     )(

time: 47.7 us -> 42.7 us (0.90)
  local copies, waits for them, and re-layouts: 9.7 us -> 3.24 us
  Pallas kernels: 37 us -> 38.6 us
    unnamed x20 -> x2, local copies, waits for them, and re-layouts: 9.7 us -> 3.24 us
    pallas_call x1, Pallas kernels: 37 us -> 38.6 us  [per_device(): pl.pallas_call(functools.partial(kernel, n, owners, heads), out_shape=(ja...]
where the time goes in v3:
time: 42.7 us; the launch traced here: 42.5 us
  Pallas kernels  38.6 us (90%)
  local copies, waits for them, and re-layouts  3.24 us (8%)
  between operations  0.64 us (1%)
    pallas_call x1, Pallas kernels, per_device(): pl.pallas_call(functools.partial(kernel, n, owners, heads), out_shape=(ja...  38.6 us
    unnamed x2, local copies, waits for them, and re-layouts  3.24 us

profile of v3, /device:TPU:0, one launch (start us, length us, event | category | flops | bytes accessed | tf_op | source)
XLA Modules:
  0.0 42.5 jit_solution(9271775364036101454)
XLA Ops:
  0.6 38.6 %encoder.1 = (bf16[256,512]{1,0:T(8,128)(2,1)}, bf16[128,512]{1,0:T(8,128)(2,1)}) custom-call(bf16[256,512]{1,0:T(8,128)(2,1)} %tok_hbm.1, bf16[128,512]{1,0:T(8,128)(2,1)} %glob_hbm.1, s32[2,128]{1,0:T(2,128)} %bitcast.2, s32[1,128]{1,0:T(1,128)} %bitcast.3, bf16[2,512,1536]{2,1,0:T(8,128)(2,1)} %wqkv_hbm.1, bf16[2,512,512]{2,1,0:T(8,128)(2,1)} %wout_hbm.1, ...), custom_call_target="tpu_custom_call" | custom-call | tf_op jit(solution)/shard_map/encoder/pallas_call | solution.py:459
  39.3 1.7 %copy.13 = bf16[256,512]{1,0:T(8,128)(2,1)} copy(bf16[256,512]{1,0:T(8,128)(2,1)} %get-tuple-element.4) | data formatting | bytes 524288
  41.0 1.6 %copy.14 = bf16[128,512]{1,0:T(8,128)(2,1)} copy(bf16[128,512]{1,0:T(8,128)(2,1)} %get-tuple-element.5) | data formatting | bytes 262144

commit v4 on v3

--- a/solution.py
+++ b/solution.py
@@ -35,6 +35,14 @@
 def fold(rows):
     half = rows.shape[1] // 2
     return jnp.concatenate([rows[:, :half], rows[:, half:]], axis=0)
+
+
+def steps(first, last, body):
+    if last <= 16:
+        for i in range(first, last):
+            body(i)
+    else:
+        pl.loop(first, last)(body)
 
 
 def kernel(
@@ -58,7 +66,9 @@
 
     barrier = pltpu.get_barrier_semaphore()
 
-    @pl.loop(1, n)
+    each_peer = functools.partial(steps, 1, n)
+
+    @each_peer
     def _(r):
         pl.semaphore_signal(
             barrier, inc=1, device_id={"seq": lax.rem(me + r, n)},
@@ -113,14 +123,14 @@
             device_id={"seq": target}, device_id_type=pl.DeviceIdType.MESH,
         )
 
-    def halo_to_right(l):
+    def halo_to_right(l, c):
+        piece = pl.ds(c * BLK, BLK)
+        return remote(xa.at[l, piece], xh.at[l, piece], h_send.at[l, 0, c], h_recv.at[l, 0, c], right)
+
+    def halo_to_left(l, c):
         return remote(
-            xa.at[l, pl.ds(0, rows)], xh.at[l, pl.ds(0, rows)], h_send.at[l, 0], h_recv.at[l, 0], right
-        )
-
-    def halo_to_left(l):
-        return remote(
-            xa.at[l, pl.ds(0, rows)], xh.at[l, pl.ds(rows, rows)], h_send.at[l, 1], h_recv.at[l, 1], left
+            xa.at[l, pl.ds(c * BLK, BLK)], xh.at[l, pl.ds(rows + c * BLK, BLK)],
+            h_send.at[l, 1, c], h_recv.at[l, 1, c], left,
         )
 
     def seg_to_right():
@@ -129,25 +139,29 @@
     def seg_to_left():
         return remote(seg_own, seg_halo.at[1], seg_send.at[1], seg_recv.at[1], left)
 
-    def send_halo(l):
+    def send_halo(l, c):
         @pl.when(has_right)
         def _():
-            halo_to_right(l).start()
+            halo_to_right(l, c).start()
 
         @pl.when(has_left)
         def _():
-            halo_to_left(l).start()
-
-    def wait_halo(l):
+            halo_to_left(l, c).start()
+
+    def wait_left(l):
         @pl.when(has_left)
         def _():
-            halo_to_right(l).wait_recv()
-
+            for c in range(2):
+                halo_to_right(l, c).wait_recv()
+
+    def wait_right(l):
         @pl.when(has_right)
         def _():
-            halo_to_left(l).wait_recv()
-
-    send_halo(0)
+            for c in range(2):
+                halo_to_left(l, c).wait_recv()
+
+    for c in range(2):
+        send_halo(0, c)
 
     @pl.when(has_right)
     def _():
@@ -165,27 +179,43 @@
         else:
             pl.when(me < owners)(body)
 
-    def others(count, body):
-        if count == n:
-            @pl.loop(1, n)
-            def _(r):
-                body(lax.rem(me + r, n))
+    def rs_copy(l, target, slot):
+        return remote(
+            rs_src.at[l, target], rs_buf.at[l, slot], rs_send.at[l], rs_recv.at[l], target
+        )
+
+    def rs_start(l):
+        def send(r):
+            target = lax.rem(me + r, n)
+            if all_own:
+                rs_copy(l, target, r - 1).start()
+            else:
+                @pl.when(target < owners)
+                def _():
+                    rs_copy(l, target, r - 1).start()
+
+        steps(1, n, send)
+
+    def ag_start(l):
+        def send(r):
+            mine = ag_buf.at[l, me]
+            remote(mine, mine, ag_send.at[l], ag_recv.at[l], lax.rem(me + r, n)).start()
+
+        steps(1, n, send)
+
+    def drain(ref, sem):
+        pltpu.make_async_copy(ref, ref, sem).wait()
+
+    def drain_sent(l):
+        for first in range(0, n - 1, owners):
+            drain(ag_buf.at[l, pl.ds(0, min(owners, n - 1 - first))], ag_send.at[l])
+
+    def by_owner(body):
+        if all_own:
+            body(owners - 1)
         else:
-            @pl.loop(0, count)
-            def _(r):
-                @pl.when(r != me)
-                def _():
-                    body(r)
-
-    def rs_copy(l, target, source):
-        return remote(
-            rs_src.at[l, target], rs_buf.at[l, source], rs_send.at[l, target], rs_recv.at[l, source], target
-        )
-
-    def ag_copy(l, target, source):
-        return remote(
-            ag_buf.at[l, source], ag_buf.at[l, source], ag_send.at[l, target], ag_recv.at[l, source], target
-        )
+            pl.when(me < owners)(lambda: body(owners - 1))
+            pl.when(me >= owners)(lambda: body(owners))
 
     for copy in small_in:
         copy.wait()
@@ -323,11 +353,11 @@
         for o in range(owners):
             cut = slice(o * GROWS, (o + 1) * GROWS)
             rs_src[l, o] = jnp.concatenate([upper[cut], lower[cut]], axis=0).astype(BF16)
-        others(owners, lambda peer: rs_copy(l, peer, me).start())
+        rs_start(l)
 
     def combine(l):
-        rs_buf[l, me] = rs_src[l, me]
-        others(n, lambda peer: rs_copy(l, me, peer).wait_recv())
+        rs_buf[l, n - 1] = rs_src[l, me]
+        drain(rs_buf.at[l, pl.ds(0, n - 1)], rs_recv.at[l])
         half = width // 2
         got = rs_buf[l].astype(F32)
         upper = got[:, :GROWS, :]
@@ -344,10 +374,10 @@
         if l + 1 < LAYERS:
             new = norm_rows(new, gg_ref[l + 1 : l + 2, :])
         ag_buf[l, me] = fold(new).astype(BF16)
-        others(n, lambda peer: ag_copy(l, peer, me).start())
+        ag_start(l)
 
     def gathered(l):
-        others(owners, lambda peer: ag_copy(l, me, peer).wait_recv())
+        by_owner(lambda slots: drain(ag_buf.at[l, pl.ds(0, slots)], ag_recv.at[l]))
         got = ag_buf[l].astype(F32)
         half = width // 2
         return jnp.concatenate(
@@ -378,7 +408,6 @@
             project_global(l)
             global_part(l)
 
-        wait_halo(l)
         if l == 0:
             @pl.when(has_left)
             def _():
@@ -394,7 +423,9 @@
                         k_far, side * span + part * BLK, marks(seg_halo[side, part : part + 1, :])
                     )
 
+        wait_left(l)
         put_keys(l, xh[l, 0:rows, :], (k_far, v_far, 0))
+        wait_right(l)
         put_keys(l, xh[l, rows : 2 * rows, :], (k_far, v_far, span))
         only_owner(functools.partial(combine, l))
 
@@ -409,18 +440,18 @@
                 fb = jnp.exp(top_b - top)
                 inv = 1.0 / (l_a[rb, p] * fa + total_b * fb)
                 value = o_a[rb, p] * (fa * inv) + value_b * (fb * inv)
-                lanes = slice(rb * BLK, (rb + 1) * BLK)
-                mixt[p * BLK : p * BLK + head_dim, lanes] = value[:, :BLK]
-                mixt[p * BLK + head_dim : (p + 1) * BLK, lanes] = value[:, BLK:]
-
-        mix = jnp.transpose(mixt[...]).astype(BF16)
-        new = stream[...] + jnp.dot(mix, wout[l], preferred_element_type=F32)
-        if l + 1 < LAYERS:
-            stream[...] = new
-            xa[l + 1, 0:rows, :] = norm_rows(new, gl_ref[l + 1 : l + 2, :]).astype(BF16)
-            send_halo(l + 1)
-        else:
-            out_ref[...] = new.astype(BF16)
+                mixt[rb, p * BLK : p * BLK + head_dim, :] = value[:, :BLK]
+                mixt[rb, p * BLK + head_dim : (p + 1) * BLK, :] = value[:, BLK:]
+
+            here = slice(rb * BLK, (rb + 1) * BLK)
+            mix = jnp.transpose(mixt[rb].astype(BF16))
+            new = stream[here, :] + jnp.dot(mix, wout[l], preferred_element_type=F32)
+            if l + 1 < LAYERS:
+                stream[here, :] = new
+                xa[l + 1, here, :] = norm_rows(new, gl_ref[l + 1 : l + 2, :]).astype(BF16)
+                send_halo(l + 1, rb)
+            else:
+                out_ref[here, :] = new.astype(BF16)
 
     gout_ref[...] = gathered(LAYERS - 1)
 
@@ -428,17 +459,32 @@
     def _():
         seg_to_right().wait_send()
         for l in range(LAYERS):
-            halo_to_right(l).wait_send()
+            for c in range(2):
+                halo_to_right(l, c).wait_send()
 
     @pl.when(has_left)
     def _():
         seg_to_left().wait_send()
         for l in range(LAYERS):
-            halo_to_left(l).wait_send()
+            for c in range(2):
+                halo_to_left(l, c).wait_send()
 
     for l in range(LAYERS):
-        others(owners, lambda peer: rs_copy(l, peer, me).wait_send())
-        only_owner(lambda: others(n, lambda peer: ag_copy(l, peer, me).wait_send()))
+        by_owner(lambda slots: drain(rs_src.at[l, pl.ds(0, slots)], rs_send.at[l]))
+        only_owner(lambda: drain_sent(l))
+
+
+def hand_on(a_ref, b_ref, a_out, b_out, sems):
+    half = a_ref.shape[0] // 2
+    copies = [
+        pltpu.make_async_copy(a_ref.at[pl.ds(0, half)], a_out.at[pl.ds(0, half)], sems.at[0]),
+        pltpu.make_async_copy(a_ref.at[pl.ds(half, half)], a_out.at[pl.ds(half, half)], sems.at[1]),
+        pltpu.make_async_copy(b_ref, b_out, sems.at[2]),
+    ]
+    for copy in copies:
+        copy.start()
+    for copy in copies:
+        copy.wait()
 
 
 def per_device(n, tokens, globals_in, seg_ids, table, w_qkv, w_out, gain_local, gain_global, seg_bias):
@@ -456,7 +502,7 @@
     half = width // 2
     pairs, wide, head_dim = heads // 2, 2 * BLK, width // heads
     assert 2 * head_dim == BLK
-    return pl.pallas_call(
+    local, shared = pl.pallas_call(
         functools.partial(kernel, n, owners, heads),
         out_shape=(
             jax.ShapeDtypeStruct((rows, width), BF16),
@@ -488,7 +534,7 @@
             V((2, pairs, head_dim, wide), F32),
             V((2, pairs, 1, wide), F32),
             V((2, pairs, 1, wide), F32),
-            V((width, rows), F32),
+            V((2, width, BLK), F32),
             V((rows, width), F32),
             V((gcount, width), F32),
             V((GROWS, width), F32),
@@ -498,12 +544,12 @@
             dma((8 + LAYERS,)),
             dma((2,)),
             dma((2,)),
-            dma((LAYERS, 2)),
-            dma((LAYERS, 2)),
-            dma((LAYERS, owners)),
-            dma((LAYERS, n)),
-            dma((LAYERS, n)),
-            dma((LAYERS, owners)),
+            dma((LAYERS, 2, 2)),
+            dma((LAYERS, 2, 2)),
+            dma((LAYERS,)),
+            dma((LAYERS,)),
+            dma((LAYERS,)),
+            dma((LAYERS,)),
         ],
         compiler_params=pltpu.CompilerParams(
             collective_id=0, has_side_effects=True, vmem_limit_bytes=VMEM_BYTES
@@ -513,6 +559,18 @@
         tokens, globals_in, seg_ids.reshape(2, BLK), table.reshape(1, BLK),
         w_qkv, w_out, gain_local, gain_global, seg_bias,
     )
+    return pl.pallas_call(
+        hand_on,
+        out_shape=(
+            jax.ShapeDtypeStruct(local.shape, BF16),
+            jax.ShapeDtypeStruct(shared.shape, BF16),
+        ),
+        in_specs=[hbm, hbm],
+        out_specs=(hbm, hbm),
+        scratch_shapes=[dma((3,))],
+        compiler_params=pltpu.CompilerParams(vmem_limit_bytes=VMEM_BYTES),
+        name="hand_on",
+    )(local, shared)
 
 
 def solution(mesh):

time: 42.7 us -> 51.5 us (1.21)
  Pallas kernels: 38.6 us -> 50.5 us
  local copies, waits for them, and re-layouts: 3.24 us -> 0 us
    pallas_call x0 -> x1, Pallas kernels: none -> 13 us  [per_device(): pl.pallas_call(hand_on, out_shape=(jax.ShapeDtypeStruct(local.shape, BF16...]
    unnamed x2 -> x0, local copies, waits for them, and re-layouts: 3.24 us -> none
    pallas_call x1, Pallas kernels: 38.6 us -> 37.5 us  [per_device(): pl.pallas_call(functools.partial(kernel, n, owners, heads), out_shape=(ja...]
where the time goes in v4:
time: 51.5 us; the launch traced here: 51.3 us
  Pallas kernels  50.5 us (98%)
  between operations  0.8 us (2%)
    pallas_call x1, Pallas kernels, per_device(): pl.pallas_call(functools.partial(kernel, n, owners, heads), out_shape=(ja...  37.5 us
    pallas_call x1, Pallas kernels, per_device(): pl.pallas_call(hand_on, out_shape=(jax.ShapeDtypeStruct(local.shape, BF16...  13 us

profile of v4, /device:TPU:0, one launch (start us, length us, event | category | flops | bytes accessed | tf_op | source)
XLA Modules:
  0.0 51.3 jit_solution(9625471150464255884)
XLA Ops:
  0.6 37.5 %encoder.1 = (bf16[256,512]{1,0:T(8,128)(2,1)}, bf16[128,512]{1,0:T(8,128)(2,1)}) custom-call(bf16[256,512]{1,0:T(8,128)(2,1)} %tok_hbm.1, bf16[128,512]{1,0:T(8,128)(2,1)} %glob_hbm.1, s32[2,128]{1,0:T(2,128)} %bitcast.2, s32[1,128]{1,0:T(1,128)} %bitcast.3, bf16[2,512,1536]{2,1,0:T(8,128)(2,1)} %wqkv_hbm.1, bf16[2,512,512]{2,1,0:T(8,128)(2,1)} %wout_hbm.1, ...), custom_call_target="tpu_custom_call" | custom-call | tf_op jit(solution)/shard_map/encoder/pallas_call | solution.py:505
  38.1 13.0 %hand_on.1 = (bf16[256,512]{1,0:T(8,128)(2,1)}, bf16[128,512]{1,0:T(8,128)(2,1)}) custom-call(bf16[256,512]{1,0:T(8,128)(2,1)} %get-tuple-element.4.a_ref, bf16[128,512]{1,0:T(8,128)(2,1)} %get-tuple-element.5.b_ref), custom_call_target="tpu_custom_call" | custom-call | tf_op jit(solution)/shard_map/hand_on/pallas_call | solution.py:562

commit v5 on v4

--- a/solution.py
+++ b/solution.py
@@ -423,11 +423,26 @@
                         k_far, side * span + part * BLK, marks(seg_halo[side, part : part + 1, :])
                     )
 
-        wait_left(l)
-        put_keys(l, xh[l, 0:rows, :], (k_far, v_far, 0))
-        wait_right(l)
-        put_keys(l, xh[l, rows : 2 * rows, :], (k_far, v_far, span))
-        only_owner(functools.partial(combine, l))
+        def take_left():
+            wait_left(l)
+            put_keys(l, xh[l, 0:rows, :], (k_far, v_far, 0))
+
+        def take_right():
+            wait_right(l)
+            put_keys(l, xh[l, rows : 2 * rows, :], (k_far, v_far, span))
+
+        @pl.when(lax.rem(me, 2) == 0)
+        def _():
+            take_right()
+            take_left()
+
+        @pl.when(lax.rem(me, 2) == 1)
+        def _():
+            take_left()
+            take_right()
+
+        if l + 1 == LAYERS:
+            only_owner(functools.partial(combine, l))
 
         for rb in range(2):
             for p in range(pairs):
@@ -450,6 +465,8 @@
                 stream[here, :] = new
                 xa[l + 1, here, :] = norm_rows(new, gl_ref[l + 1 : l + 2, :]).astype(BF16)
                 send_halo(l + 1, rb)
+                if rb == 0:
+                    only_owner(functools.partial(combine, l))
             else:
                 out_ref[here, :] = new.astype(BF16)
 
@@ -474,16 +491,22 @@
         only_owner(lambda: drain_sent(l))
 
 
-def hand_on(a_ref, b_ref, a_out, b_out, sems):
+def hand_on(a_ref, b_ref, a_out, b_out, a_mid, b_mid, sems):
     half = a_ref.shape[0] // 2
-    copies = [
-        pltpu.make_async_copy(a_ref.at[pl.ds(0, half)], a_out.at[pl.ds(0, half)], sems.at[0]),
-        pltpu.make_async_copy(a_ref.at[pl.ds(half, half)], a_out.at[pl.ds(half, half)], sems.at[1]),
-        pltpu.make_async_copy(b_ref, b_out, sems.at[2]),
+    first, second = pl.ds(0, half), pl.ds(half, half)
+    parts = [
+        (a_ref.at[first], a_mid.at[first], a_out.at[first]),
+        (a_ref.at[second], a_mid.at[second], a_out.at[second]),
+        (b_ref, b_mid, b_out),
     ]
-    for copy in copies:
+    reads = [pltpu.make_async_copy(s, m, sems.at[0, i]) for i, (s, m, _) in enumerate(parts)]
+    writes = [pltpu.make_async_copy(m, d, sems.at[1, i]) for i, (_, m, d) in enumerate(parts)]
+    for copy in reads:
         copy.start()
-    for copy in copies:
+    for read, write in zip(reads, writes):
+        read.wait()
+        write.start()
+    for copy in writes:
         copy.wait()
 
 
@@ -567,7 +590,7 @@
         ),
         in_specs=[hbm, hbm],
         out_specs=(hbm, hbm),
-        scratch_shapes=[dma((3,))],
+        scratch_shapes=[V(local.shape, BF16), V(shared.shape, BF16), dma((2, 3))],
         compiler_params=pltpu.CompilerParams(vmem_limit_bytes=VMEM_BYTES),
         name="hand_on",
     )(local, shared)

time: 51.5 us -> 41.4 us (0.80)
  Pallas kernels: 50.5 us -> 40.5 us
    pallas_call x1, Pallas kernels: 13 us -> 1.74 us  [per_device(): pl.pallas_call(hand_on, out_shape=(jax.ShapeDtypeStruct(local.shape, BF16...]
    pallas_call x1, Pallas kernels: 37.5 us -> 38.8 us  [per_device(): pl.pallas_call(functools.partial(kernel, n, owners, heads), out_shape=(ja...]
where the time goes in v5:
time: 41.4 us; the launch traced here: 41.3 us
  Pallas kernels  40.5 us (98%)
  between operations  0.8 us (2%)
    pallas_call x1, Pallas kernels, per_device(): pl.pallas_call(functools.partial(kernel, n, owners, heads), out_shape=(ja...  38.8 us
    pallas_call x1, Pallas kernels, per_device(): pl.pallas_call(hand_on, out_shape=(jax.ShapeDtypeStruct(local.shape, BF16...  1.74 us

profile of v5, /device:TPU:0, one launch (start us, length us, event | category | flops | bytes accessed | tf_op | source)
XLA Modules:
  0.0 41.3 jit_solution(1834968295639048642)
XLA Ops:
  0.6 38.8 %encoder.1 = (bf16[256,512]{1,0:T(8,128)(2,1)}, bf16[128,512]{1,0:T(8,128)(2,1)}) custom-call(bf16[256,512]{1,0:T(8,128)(2,1)} %tok_hbm.1, bf16[128,512]{1,0:T(8,128)(2,1)} %glob_hbm.1, s32[2,128]{1,0:T(2,128)} %bitcast.2, s32[1,128]{1,0:T(1,128)} %bitcast.3, bf16[2,512,1536]{2,1,0:T(8,128)(2,1)} %wqkv_hbm.1, bf16[2,512,512]{2,1,0:T(8,128)(2,1)} %wout_hbm.1, ...), custom_call_target="tpu_custom_call" | custom-call | tf_op jit(solution)/shard_map/encoder/pallas_call | solution.py:528
  39.4 1.7 %hand_on.1 = (bf16[256,512]{1,0:T(8,128)(2,1)}, bf16[128,512]{1,0:T(8,128)(2,1)}) custom-call(bf16[256,512]{1,0:T(8,128)(2,1)} %get-tuple-element.4.a_ref, bf16[128,512]{1,0:T(8,128)(2,1)} %get-tuple-element.5.b_ref), custom_call_target="tpu_custom_call" | custom-call | tf_op jit(solution)/shard_map/hand_on/pallas_call | solution.py:585

commit v6 on v5

--- a/solution.py
+++ b/solution.py
@@ -289,14 +289,14 @@
         spread[i] = jnp.where(hit, 1.0, 0.0).astype(F32).astype(BF16)
 
     def put_keys(l, x, *places):
-        count = x.shape[0]
         k = jnp.dot(x, wqkv[l, :, width : 2 * width], preferred_element_type=F32).astype(BF16)
         v = jnp.dot(x, wqkv[l, :, 2 * width : 3 * width], preferred_element_type=F32).astype(BF16)
         v = jnp.transpose(v)
-        for k_ref, v_ref, at in places:
+        for lo, size, k_ref, v_ref, at in places:
             for p in range(pairs):
-                k_ref[at : at + count, p * wide : p * wide + BLK] = k[:, p * BLK : (p + 1) * BLK]
-                v_ref[p, 0:BLK, at : at + count] = v[p * BLK : (p + 1) * BLK]
+                cols = slice(p * BLK, (p + 1) * BLK)
+                k_ref[at : at + size, p * wide : p * wide + BLK] = k[lo : lo + size, cols]
+                v_ref[p, 0:BLK, at : at + size] = v[cols, lo : lo + size]
 
     def put_queries(l, x, first):
         q = jnp.dot(x, wqkv[l, :, 0:width], preferred_element_type=F32)
@@ -311,12 +311,12 @@
     def project_local(l):
         x = xa[l, 0:rows, :]
         put_queries(l, x, 0)
-        put_keys(l, x, (k_own, v_own, 0))
+        put_keys(l, x, (0, rows, k_own, v_own, 0))
 
     def project_global(l):
         x = xa[l, rows : rows + gcount, :]
         put_queries(l, x, 2)
-        put_keys(l, x, (k_own, v_own, rows), (k_far, v_far, rows))
+        put_keys(l, x, (0, gcount, k_own, v_own, rows), (0, gcount, k_far, v_far, rows))
 
     def attend(l, p, rb, k_ref, v_ref, k0, count, masked=False):
         s = jnp.dot(
@@ -395,8 +395,8 @@
     for l in range(LAYERS):
         if l == 0:
             w_in[0].wait()
-            project_global(0)
-            project_local(0)
+            put_queries(0, xa[0], 0)
+            put_keys(0, xa[0], (0, span, k_own, v_own, 0), (rows, gcount, k_far, v_far, rows))
             global_part(0)
             near_part(0)
             wout_in.wait()
@@ -423,26 +423,10 @@
                         k_far, side * span + part * BLK, marks(seg_halo[side, part : part + 1, :])
                     )
 
-        def take_left():
-            wait_left(l)
-            put_keys(l, xh[l, 0:rows, :], (k_far, v_far, 0))
-
-        def take_right():
-            wait_right(l)
-            put_keys(l, xh[l, rows : 2 * rows, :], (k_far, v_far, span))
-
-        @pl.when(lax.rem(me, 2) == 0)
-        def _():
-            take_right()
-            take_left()
-
-        @pl.when(lax.rem(me, 2) == 1)
-        def _():
-            take_left()
-            take_right()
-
-        if l + 1 == LAYERS:
-            only_owner(functools.partial(combine, l))
+        wait_left(l)
+        wait_right(l)
+        put_keys(l, xh[l], (0, rows, k_far, v_far, 0), (rows, rows, k_far, v_far, span))
+        only_owner(functools.partial(combine, l))
 
         for rb in range(2):
             for p in range(pairs):
@@ -465,8 +449,6 @@
                 stream[here, :] = new
                 xa[l + 1, here, :] = norm_rows(new, gl_ref[l + 1 : l + 2, :]).astype(BF16)
                 send_halo(l + 1, rb)
-                if rb == 0:
-                    only_owner(functools.partial(combine, l))
             else:
                 out_ref[here, :] = new.astype(BF16)
 

time: 41.4 us -> 40 us (0.966)
  Pallas kernels: 40.5 us -> 39.1 us
    pallas_call x1, Pallas kernels: 38.8 us -> 37.3 us  [per_device(): pl.pallas_call(functools.partial(kernel, n, owners, heads), out_shape=(ja...]
where the time goes in v6:
time: 40 us; the launch traced here: 39.9 us
  Pallas kernels  39.1 us (98%)
  between operations  0.8 us (2%)
    pallas_call x1, Pallas kernels, per_device(): pl.pallas_call(functools.partial(kernel, n, owners, heads), out_shape=(ja...  37.3 us
    pallas_call x1, Pallas kernels, per_device(): pl.pallas_call(hand_on, out_shape=(jax.ShapeDtypeStruct(local.shape, BF16...  1.74 us

profile of v6, /device:TPU:0, one launch (start us, length us, event | category | flops | bytes accessed | tf_op | source)
XLA Modules:
  0.0 39.9 jit_solution(5834744745182203589)
XLA Ops:
  0.6 37.3 %encoder.1 = (bf16[256,512]{1,0:T(8,128)(2,1)}, bf16[128,512]{1,0:T(8,128)(2,1)}) custom-call(bf16[256,512]{1,0:T(8,128)(2,1)} %tok_hbm.1, bf16[128,512]{1,0:T(8,128)(2,1)} %glob_hbm.1, s32[2,128]{1,0:T(2,128)} %bitcast.2, s32[1,128]{1,0:T(1,128)} %bitcast.3, bf16[2,512,1536]{2,1,0:T(8,128)(2,1)} %wqkv_hbm.1, bf16[2,512,512]{2,1,0:T(8,128)(2,1)} %wout_hbm.1, ...), custom_call_target="tpu_custom_call" | custom-call | tf_op jit(solution)/shard_map/encoder/pallas_call | solution.py:510
  38.0 1.7 %hand_on.1 = (bf16[256,512]{1,0:T(8,128)(2,1)}, bf16[128,512]{1,0:T(8,128)(2,1)}) custom-call(bf16[256,512]{1,0:T(8,128)(2,1)} %get-tuple-element.4.a_ref, bf16[128,512]{1,0:T(8,128)(2,1)} %get-tuple-element.5.b_ref), custom_call_target="tpu_custom_call" | custom-call | tf_op jit(solution)/shard_map/hand_on/pallas_call | solution.py:567
